TPU v7x, 256 devices: a whole 4x4x8 slice. The times are simulated.
256 devices in a mesh: dp: 32 (over x, y, z_lo), seq: 8 (over z_hi, core).
Axes of the slice: x: 4, y: 4, z: 8 (z_hi: 4, z_lo: 2; z = z_hi * 2 + z_lo), core: 2. Of those that a mesh axis runs over, the one named last changes fastest.
Arguments:
- qkv: bfloat16 [3, 32, 2, 512, 3072], P(None, 'dp', None, 'seq'), may hold values from -18 to 18
- cotangent: bfloat16 [32, 2, 512, 3072], P('dp', None, 'seq'), may hold values from -6 to 6
- lengths: int32 [32, 2], replicated, may hold values from 0 to 512, as said below
- target_group: int32 [32, 2], replicated, may hold values from 0 to 31, as said below
- target_slot: int32 [32, 2], replicated, may hold values from 0 to 1, as said below
Outputs:
- attended: bfloat16 [32, 2, 512, 3072], P('dp', None, 'seq')
- grad_qkv: bfloat16 [3, 32, 2, 512, 3072], P(None, 'dp', None, 'seq')
Inputs may be any that keep to these rules, and one draw needn't show every extreme that they name: Each group holds 0 to 2 clips; an empty slot has length 0, a clip has 128 to 512 tokens, and some clip has exactly 512. A move lowers the larger of the two groups' sums of squared clip lengths. `target_group`: A clip stays in its group or moves to the group one below or one above; a group sends at most one clip to each neighbour and at most one clip arrives in a group; a group that sends receives nothing; group 0 sends one clip to group 1 and the last group one to the group below it; empty slots name their own group. `target_slot`: A clip that stays keeps its slot; a moving clip lands in a slot of its destination that holds no clip before the moves; empty slots name their own slot.
All inputs are finite; a program needn't handle non-finite values.
Results may differ from a plain program's by a relative error of at most 0.0049.
Values may be sent and summed in bfloat16 or wider, within the bound.
No kernel may reach another device: no remote copies, remote signals or barrier semaphores. Data moves between devices by JAX's collectives and lax.ppermute only.
A program may use at most 64 MiB of HBM per device.

v0:
```python
import functools

import jax
import jax.numpy as jnp
from jax import lax
from jax.experimental import pallas as pl
from jax.experimental.pallas import tpu as pltpu
from jax.sharding import PartitionSpec as P

HEAD = 128
SEQ = 8
ARRAYS = 4
NEGATIVE = -1e30
LOG2E = 1.4426950408889634
CORES = 2
ORDER = (4, 5, 2, 6, 3, 7, 1)
CHUNKS = ((0, 3),)
ANY = pl.BlockSpec(memory_space=pl.ANY)
VMEM = pl.BlockSpec(memory_space=pltpu.VMEM)
SMEM = pl.BlockSpec(memory_space=pltpu.SMEM)


def partners(group):
    odd = lax.rem(group, 2)
    return group + 1 - 2 * odd, group - 1 + 2 * odd


def plan_kernel(lengths, to_group, to_slot, plan):
    groups = lengths.shape[0]
    me = lax.axis_index("dp")
    grad_source = [jnp.int32(0), jnp.int32(0)]
    out_source = []
    for slot in range(2):
        stays = (lengths[me, slot] > 0) & (to_group[me, slot] == me)
        out_source.append(jnp.where(stays, 0, 3))
    for number, other in enumerate(partners(me)):
        inside = (other >= 0) & (other < groups)
        there = jnp.clip(other, 0, groups - 1)
        kind = jnp.int32(0)
        given = jnp.int32(0)
        for slot in range(2):
            leaves = inside & (lengths[me, slot] > 0) & (to_group[me, slot] == other)
            arrives = inside & (lengths[there, slot] > 0) & (to_group[there, slot] == me)
            lands = to_slot[there, slot]
            kind = jnp.where(leaves, 1, jnp.where(arrives, 2, kind))
            given = jnp.where(leaves, slot, jnp.where(arrives, lands, given))
            grad_source[slot] = jnp.where(leaves, number + 1, grad_source[slot])
            for here in range(2):
                out_source[here] = jnp.where(arrives & (lands == here), number + 1, out_source[here])
        plan[2 * number] = kind
        plan[2 * number + 1] = given
    for slot in range(2):
        plan[4 + slot] = grad_source[slot]
        plan[6 + slot] = out_source[slot]
        plan[8 + slot] = lengths[me, slot]


def make_plan(lengths, to_group, to_slot):
    return pl.pallas_call(
        plan_kernel,
        out_shape=jax.ShapeDtypeStruct((10,), jnp.int32),
        in_specs=[SMEM] * 3,
        out_specs=SMEM,
        name="plan",
    )(lengths, to_group, to_slot)


def reached(seq, k, sign):
    chips = SEQ // CORES
    chip = (seq // CORES + sign * (k // CORES) + chips) % chips
    return chip * CORES + (seq + k) % CORES


def block_columns(k, device_width, chunk):
    other = reached(lax.axis_index("seq"), k, 1)
    start = pl.multiple_of(other * device_width + chunk[0] * HEAD, HEAD)
    return pl.ds(start, chunk[1] * HEAD)


def pack_kernel(chunk, qkv, cotangent, *refs):
    outs, (held, come, go) = refs[:SEQ], refs[SEQ:]
    device_width = qkv.shape[-1] // SEQ
    arrive = []
    for k in range(SEQ):
        columns = block_columns(k, device_width, chunk)
        arrive.append(
            (
                pltpu.make_async_copy(
                    qkv.at[:, 0, :, :, columns], held.at[k, pl.ds(0, 3)], come.at[k, 0]
                ),
                pltpu.make_async_copy(
                    cotangent.at[0, :, :, columns], held.at[k, 3], come.at[k, 1]
                ),
            )
        )
    leave = [pltpu.make_async_copy(held.at[k], outs[k], go.at[k]) for k in range(SEQ)]
    for pair in arrive:
        for copy in pair:
            copy.start()
    for pair, copy in zip(arrive, leave):
        for part in pair:
            part.wait()
        copy.start()
    for copy in leave:
        copy.wait()


def pack(qkv, cotangent, chunk):
    _, slots, rows, _ = cotangent.shape
    shape = (ARRAYS, slots, rows, chunk[1] * HEAD)
    return pl.pallas_call(
        functools.partial(pack_kernel, chunk),
        out_shape=[jax.ShapeDtypeStruct(shape, qkv.dtype)] * SEQ,
        in_specs=[ANY, ANY],
        out_specs=[ANY] * SEQ,
        scratch_shapes=[
            pltpu.VMEM((SEQ, *shape), qkv.dtype),
            pltpu.SemaphoreType.DMA((SEQ, 2)),
            pltpu.SemaphoreType.DMA((SEQ,)),
        ],
        name="pack",
    )(qkv, cotangent)


def exchange(parts, sign):
    received = list(parts)
    for k in ORDER:
        pairs = [(i, reached(i, k, sign)) for i in range(SEQ)]
        received[k] = lax.ppermute(parts[k], "seq", pairs)
    return received


def token_numbers(shape, axis):
    rows = shape[axis] // SEQ
    blocks = [reached(lax.axis_index("seq"), k, -1) for k in range(SEQ)]
    piece = shape[:axis] + (rows,) + shape[axis + 1 :]
    within = lax.broadcasted_iota(jnp.int32, piece, axis)
    return jnp.concatenate([within + block * rows for block in blocks], axis=axis)


def head_columns(head):
    return slice(head * HEAD, (head + 1) * HEAD)


def gathered(parts, array, slot, columns):
    return jnp.concatenate([part[array, slot, :, columns] for part in parts], axis=0)


def dot(a, b, a_axis, b_axis):
    return lax.dot_general(
        a, b, (((a_axis,), (b_axis,)), ((), ())), preferred_element_type=jnp.float32
    )


def scores_of(queries, keys, valid_keys):
    scores = dot(keys, queries, 1, 1) * (HEAD**-0.5 * LOG2E)
    return jnp.where(valid_keys, scores, NEGATIVE)


def forward_kernel(plan, *refs):
    parts, (out, stats, *gifts) = refs[:SEQ], refs[SEQ:]
    slots, tokens, width = out.shape
    rows = tokens // SEQ
    heads = width // HEAD
    for slot in range(slots):
        count = plan[8 + slot]

        @pl.when(count == 0)
        def _():
            out[slot] = jnp.zeros_like(out[slot])

        @pl.when(count > 0)
        def _():
            valid_keys = token_numbers((tokens, tokens), 0) < count
            valid_queries = token_numbers((tokens, HEAD), 0) < count
            for head in range(heads):
                columns = head_columns(head)
                queries, keys, values = (gathered(parts, n, slot, columns) for n in range(3))
                scores = scores_of(queries, keys, valid_keys)
                largest = jnp.max(scores, axis=0, keepdims=True)
                exponent = jnp.exp2(scores - largest)
                inverse = 1.0 / jnp.sum(exponent, axis=0, keepdims=True)
                weights = (exponent * inverse).astype(jnp.bfloat16)
                output = dot(values, weights, 0, 0).T
                output = jnp.where(valid_queries, output, 0.0).astype(jnp.bfloat16)
                out[slot, :, columns] = output
                stats[slot, 2 * head : 2 * head + 1, :] = largest
                stats[slot, 2 * head + 1 : 2 * head + 2, :] = inverse

    for number, gift in enumerate(gifts):
        for slot in range(slots):
            chosen = plan[2 * number + 1] == slot

            @pl.when((plan[2 * number] == 1) & chosen)
            def _():
                gift[...] = out[slot]

            @pl.when((plan[2 * number] == 2) & chosen)
            def _():
                for k, part in enumerate(parts):
                    gift[k * rows : (k + 1) * rows] = part[3, slot]


def forward(plan, parts):
    _, slots, rows, width = parts[0].shape
    tokens = rows * SEQ
    gift = jax.ShapeDtypeStruct((tokens, width), jnp.bfloat16)
    return pl.pallas_call(
        forward_kernel,
        out_shape=[
            jax.ShapeDtypeStruct((slots, tokens, width), jnp.bfloat16),
            jax.ShapeDtypeStruct((slots, 8, tokens), jnp.float32),
            gift,
            gift,
        ],
        in_specs=[SMEM] + [VMEM] * SEQ,
        out_specs=[VMEM] * 4,
        compiler_params=pltpu.CompilerParams(vmem_limit_bytes=40 << 20),
        name="forward",
    )(plan, *parts)


def backward_kernel(plan, *refs):
    parts, (home_out, stats, even, odd), outs = refs[:SEQ], refs[SEQ : SEQ + 4], refs[SEQ + 4 :]
    slots, tokens, width = home_out.shape
    rows = tokens // SEQ
    heads = width // HEAD
    for slot in range(slots):
        count = plan[8 + slot]
        for choice, source in ((0, home_out.at[slot]), (1, even), (2, odd)):

            @pl.when(plan[6 + slot] == choice)
            def _():
                for k, out in enumerate(outs):
                    out[0, slot] = source[k * rows : (k + 1) * rows]

        @pl.when(plan[6 + slot] == 3)
        def _():
            for out in outs:
                out[0, slot] = jnp.zeros_like(out[0, slot])

        @pl.when(count == 0)
        def _():
            for out in outs:
                for array in range(1, ARRAYS):
                    out[array, slot] = jnp.zeros_like(out[array, slot])

        @pl.when(count > 0)
        def _():
            source = plan[4 + slot]
            valid_keys = token_numbers((tokens, tokens), 0) < count
            valid_queries = token_numbers((tokens, HEAD), 0) < count
            factor = HEAD**-0.5
            for head in range(heads):
                columns = head_columns(head)
                queries, keys, values, own = (
                    gathered(parts, n, slot, columns) for n in range(ARRAYS)
                )
                moved = jnp.where(source == 1, even[:, columns], odd[:, columns])
                upstream = jnp.where(source == 0, own, moved)
                upstream = jnp.where(valid_queries, upstream, jnp.zeros_like(upstream))
                scores = scores_of(queries, keys, valid_keys)
                largest = stats[slot, 2 * head : 2 * head + 1, :]
                inverse = stats[slot, 2 * head + 1 : 2 * head + 2, :]
                weights = jnp.exp2(scores - largest) * inverse
                grad_values = dot(weights.astype(jnp.bfloat16), upstream, 1, 0)
                grad_weights = dot(values, upstream, 1, 1)
                inner = jnp.sum(grad_weights * weights, axis=0, keepdims=True)
                score_grad = (weights * (grad_weights - inner)).astype(jnp.bfloat16)
                grad_queries = dot(keys, score_grad, 0, 0).T * factor
                grad_keys = dot(score_grad, queries, 1, 0) * factor
                for n, grad in enumerate((grad_queries, grad_keys, grad_values)):
                    grad = grad.astype(jnp.bfloat16)
                    for k, out in enumerate(outs):
                        out[1 + n, slot, :, columns] = grad[k * rows : (k + 1) * rows]


def backward(plan, parts, home_out, stats, even, odd):
    return pl.pallas_call(
        backward_kernel,
        out_shape=[jax.ShapeDtypeStruct(parts[0].shape, jnp.bfloat16)] * SEQ,
        in_specs=[SMEM] + [VMEM] * (SEQ + 4),
        out_specs=[VMEM] * SEQ,
        compiler_params=pltpu.CompilerParams(vmem_limit_bytes=48 << 20),
        name="backward",
    )(plan, *parts, home_out, stats, even, odd)


def unpack_kernel(chunk, *refs):
    parts, (attended, grads, sem) = refs[:SEQ], refs[-3:]
    device_width = grads.shape[-1] // SEQ
    copies = []
    for k, part in enumerate(parts):
        columns = block_columns(k, device_width, chunk)
        copies += [
            pltpu.make_async_copy(part.at[0], attended.at[0, :, :, columns], sem.at[k, 0]),
            pltpu.make_async_copy(
                part.at[pl.ds(1, 3)], grads.at[:, 0, :, :, columns], sem.at[k, 1]
            ),
        ]
    for copy in copies:
        copy.start()
    for copy in copies:
        copy.wait()


def unpack(parts, chunk, device_heads, filled=()):
    _, slots, rows, _ = parts[0].shape
    features = device_heads * HEAD * SEQ
    return pl.pallas_call(
        functools.partial(unpack_kernel, chunk),
        out_shape=[
            jax.ShapeDtypeStruct((1, slots, rows, features), jnp.bfloat16),
            jax.ShapeDtypeStruct((3, 1, slots, rows, features), jnp.bfloat16),
        ],
        in_specs=[VMEM] * SEQ + [ANY] * len(filled),
        out_specs=[ANY, ANY],
        input_output_aliases={SEQ + n: n for n in range(len(filled))},
        scratch_shapes=[pltpu.SemaphoreType.DMA((SEQ, 2))],
        name="unpack",
    )(*parts, *filled)


def swap(kind, gift, first, groups):
    pairs = []
    for low in range(first, groups - 1, 2):
        pairs += [(low, low + 1), (low + 1, low)]
    return lax.cond(
        kind > 0, lambda gift: lax.ppermute(gift, "dp", pairs), lambda gift: gift, gift
    )


def after(value, *others):
    return lax.optimization_barrier((value, *others))[0]


def on_device(qkv, cotangent, lengths, to_group, to_slot):
    groups = lengths.shape[0]
    device_heads = qkv.shape[-1] // (HEAD * SEQ)
    plan = make_plan(lengths, to_group, to_slot)
    packed = [pack(qkv, cotangent, chunk) for chunk in CHUNKS]
    arrived = [exchange(parts, 1) for parts in packed]
    returned = []
    for parts in arrived:
        home_out, stats, *gifts = forward(plan, parts)
        even, odd = (swap(plan[2 * n], gifts[n], n, groups) for n in range(2))
        returned.append(exchange(backward(plan, parts, home_out, stats, even, odd), -1))
    results = ()
    for parts, chunk in zip(returned, CHUNKS):
        results = unpack(parts, chunk, device_heads, results)
    return tuple(results)


def solution(mesh):
    in_specs = (P(None, "dp", None, "seq", None), P("dp", None, "seq", None), P(), P(), P())
    out_specs = (P("dp", None, "seq", None), P(None, "dp", None, "seq", None))
    return jax.shard_map(
        on_device, mesh=mesh, in_specs=in_specs, out_specs=out_specs, check_vma=False
    )
```

profile of v0, /device:TPU:33, one launch (start us, length us, event | category | flops | bytes accessed | tf_op | source)
XLA Modules:
  0.0 193.1 jit_solution(12889700105261030994)
XLA Ops:
  0.7 2.9 %pack.1 = (bf16[4,2,64,384]{3,2,1,0:T(8,128)(2,1)}, bf16[4,2,64,384]{3,2,1,0:T(8,128)(2,1)}, bf16[4,2,64,384]{3,2,1,0:T(8,128)(2,1)}, bf16[4,2,64,384]{3,2,1,0:T...) custom-call(bf16[3,1,2,64,3072]{4,3,2,1,0:T(8,128)(2,1)} %qkv.1, ...), custom_call_target="tpu_custom_call" | custom-call | tf_op jit(solution)/shard_map/pack/pallas_call | solution.py:111
  3.6 0.8 collective-permute-start.2
  4.3 3.0 %collective-permute-start.3 = (bf16[4,2,64,384]{3,2,1,0:T(8,128)(2,1)}, bf16[4,2,64,384]{3,2,1,0:T(8,128)(2,1)S(1)}, u32[]{:S(2)}, u32[]{:S(2)}) collective-permute-start(bf16[4,2,64,384]{3,2,1,0:T(8,128)(2,1)} %get-tuple-element.34), channel_id=1, source_target_pairs={{0,2},{1,3},{2,4},{3,5},{4,6},{5,7},{6,0},{7,1},{8,10},{9,11},{10,... | collective-permute-start | bytes 1179656 | tf_op jit(solution)/shard_map/ppermute | solution.py:129
  7.3 3.5 %collective-permute-start.4 = (bf16[4,2,64,384]{3,2,1,0:T(8,128)(2,1)}, bf16[4,2,64,384]{3,2,1,0:T(8,128)(2,1)S(1)}, u32[]{:S(2)}, u32[]{:S(2)}) collective-permute-start(bf16[4,2,64,384]{3,2,1,0:T(8,128)(2,1)} %get-tuple-element.35), channel_id=1, source_target_pairs={{0,3},{1,2},{2,5},{3,4},{4,7},{5,6},{6,1},{7,0},{8,11},{9,10},{10,... | collective-permute-start | bytes 1179656 | tf_op jit(solution)/shard_map/ppermute | solution.py:129
  11.6 5.0 %collective-permute-start.6 = (bf16[4,2,64,384]{3,2,1,0:T(8,128)(2,1)}, bf16[4,2,64,384]{3,2,1,0:T(8,128)(2,1)S(1)}, u32[]{:S(2)}, u32[]{:S(2)}) collective-permute-start(bf16[4,2,64,384]{3,2,1,0:T(8,128)(2,1)} %get-tuple-element.37), channel_id=1, source_target_pairs={{0,5},{1,4},{2,7},{3,6},{4,1},{5,0},{6,3},{7,2},{8,13},{9,12},{10,... | collective-permute-start | bytes 1179656 | tf_op jit(solution)/shard_map/ppermute | solution.py:129
  16.8 22.6 %collective-permute-done.3.refs_2_ = bf16[4,2,64,384]{3,2,1,0:T(8,128)(2,1)S(1)} collective-permute-done((bf16[4,2,64,384]{3,2,1,0:T(8,128)(2,1)}, bf16[4,2,64,384]{3,2,1,0:T(8,128)(2,1)S(1)}, u32[]{:S(2)}, u32[]{:S(2)}) %collective-permute-start.3) | collective-permute-done | bytes 393248 | tf_op jit(solution)/shard_map/ppermute | solution.py:129
  39.4 3.9 %collective-permute-start.8 = (bf16[4,2,64,384]{3,2,1,0:T(8,128)(2,1)}, bf16[4,2,64,384]{3,2,1,0:T(8,128)(2,1)S(1)}, u32[]{:S(2)}, u32[]{:S(2)}) collective-permute-start(bf16[4,2,64,384]{3,2,1,0:T(8,128)(2,1)} %get-tuple-element.39), channel_id=1, source_target_pairs={{0,7},{1,6},{2,1},{3,0},{4,3},{5,2},{6,5},{7,4},{8,15},{9,14},{10,... | collective-permute-start | bytes 1179656 | tf_op jit(solution)/shard_map/ppermute | solution.py:129
  45.4 2.0 %plan.1 = s32[10]{0:T(128)} custom-call(s32[32,2]{1,0:T(8,128)} %copy.7.lengths, s32[32,2]{1,0:T(8,128)} %copy.8.to_group, s32[32,2]{1,0:T(8,128)} %copy.9.to_slot), custom_call_target="tpu_custom_call" | custom-call | tf_op jit(solution)/shard_map/plan/pallas_call | solution.py:59
  47.4 1.3 fusion
  50.1 12.7 %collective-permute-done.4.refs_3_ = bf16[4,2,64,384]{3,2,1,0:T(8,128)(2,1)S(1)} collective-permute-done((bf16[4,2,64,384]{3,2,1,0:T(8,128)(2,1)}, bf16[4,2,64,384]{3,2,1,0:T(8,128)(2,1)S(1)}, u32[]{:S(2)}, u32[]{:S(2)}) %collective-permute-start.4) | collective-permute-done | bytes 393248 | tf_op jit(solution)/shard_map/ppermute | solution.py:129
  62.8 2.4 %collective-permute-done.8.refs_7_ = bf16[4,2,64,384]{3,2,1,0:T(8,128)(2,1)S(1)} collective-permute-done((bf16[4,2,64,384]{3,2,1,0:T(8,128)(2,1)}, bf16[4,2,64,384]{3,2,1,0:T(8,128)(2,1)S(1)}, u32[]{:S(2)}, u32[]{:S(2)}) %collective-permute-start.8) | collective-permute-done | bytes 393248 | tf_op jit(solution)/shard_map/ppermute | solution.py:129
  65.3 1.1 copy-done
  67.1 3.5 %forward.1 = (bf16[2,512,384]{2,1,0:T(8,128)(2,1)S(1)}, f32[2,8,512]{2,1,0:T(8,128)S(1)}, bf16[512,384]{1,0:T(8,128)(2,1)}, bf16[512,384]{1,0:T(8,128)(2,1)}) custom-call(s32[10]{0:T(128)S(1)} %copy-done.5, bf16[4,2,64,384]{3,2,1,0:T(8,128)(2,1)S(1)} %copy-done, bf16[4,2,64,384]{3,2,1,0:T(8,128)(2,1)S(1)} %collective-permute-done.2.refs_1_, ...), custom_call_target="tpu_custom_call" | custom-call | tf_op jit(solution)/shard_map/forward/pallas_call | solution.py:208
  70.6 0.9 copy-done.3
  71.5 30.1 %conditional.2 = (bf16[512,384]{1,0:T(8,128)(2,1)}) conditional(s32[]{:T(128)} %bitcast, bf16[512,384]{1,0:T(8,128)(2,1)} %get-tuple-element.42, bf16[512,384]{1,0:T(8,128)(2,1)} %get-tuple-element.42), branch_computations={%region_0.0_spmd, %region_1.0_spmd} | conditional | bytes 2359344 | solution.py:328
  71.5 20.0 %collective-permute-start = (bf16[512,384]{1,0:T(8,128)(2,1)}, bf16[512,384]{1,0:T(8,128)(2,1)S(1)}, u32[]{:S(2)}, u32[]{:S(2)}) collective-permute-start(bf16[512,384]{1,0:T(8,128)(2,1)} %param.1), channel_id=1, source_target_pairs={{0,8},{8,0},{16,24},{24,16},{32,40},{40,32},{48,56},{56,48},{64,72... | collective-permute-start | bytes 1179656 | tf_op jit(solution)/shard_map/cond/branch_1_fun/ppermute | solution.py:329
  91.4 9.4 %collective-permute-done = bf16[512,384]{1,0:T(8,128)(2,1)S(1)} collective-permute-done((bf16[512,384]{1,0:T(8,128)(2,1)}, bf16[512,384]{1,0:T(8,128)(2,1)S(1)}, u32[]{:S(2)}, u32[]{:S(2)}) %collective-permute-start) | collective-permute-done | bytes 393248 | tf_op jit(solution)/shard_map/cond/branch_1_fun/ppermute | solution.py:329
  100.8 0.8 copy.11
  101.6 4.8 %backward.1 = (bf16[4,2,64,384]{3,2,1,0:T(8,128)(2,1)S(1)}, bf16[4,2,64,384]{3,2,1,0:T(8,128)(2,1)S(1)}, bf16[4,2,64,384]{3,2,1,0:T(8,128)(2,1)S(1)}, bf16[4,2,6...) custom-call(s32[10]{0:T(128)S(1)} %copy-done.6, ...), custom_call_target="tpu_custom_call" | custom-call | tf_op jit(solution)/shard_map/backward/pallas_call | solution.py:279
  106.4 0.8 copy-done.4
  107.1 0.9 collective-permute-start.9
  108.1 1.9 collective-permute-start.10
  110.0 2.3 %collective-permute-start.11 = (bf16[4,2,64,384]{3,2,1,0:T(8,128)(2,1)S(1)}, bf16[4,2,64,384]{3,2,1,0:T(8,128)(2,1)S(1)}, u32[]{:S(2)}, u32[]{:S(2)}) collective-permute-start(bf16[4,2,64,384]{3,2,1,0:T(8,128)(2,1)S(1)} %get-tuple-element.47), channel_id=1, source_target_pairs={{0,7},{1,6},{2,1},{3,0},{4,3},{5,2},{6,5},{7,4},{8,15},{9,14},{10,... | collective-permute-start | bytes 1179656 | tf_op jit(solution)/shard_map/ppermute | solution.py:129
  112.3 2.3 %collective-permute-start.12 = (bf16[4,2,64,384]{3,2,1,0:T(8,128)(2,1)S(1)}, bf16[4,2,64,384]{3,2,1,0:T(8,128)(2,1)S(1)}, u32[]{:S(2)}, u32[]{:S(2)}) collective-permute-start(bf16[4,2,64,384]{3,2,1,0:T(8,128)(2,1)S(1)} %get-tuple-element.48), channel_id=1, source_target_pairs={{0,4},{1,5},{2,6},{3,7},{4,0},{5,1},{6,2},{7,3},{8,12},{9,13},{10,... | collective-permute-start | bytes 1179656 | tf_op jit(solution)/shard_map/ppermute | solution.py:129
  114.6 3.5 %collective-permute-start.13 = (bf16[4,2,64,384]{3,2,1,0:T(8,128)(2,1)S(1)}, bf16[4,2,64,384]{3,2,1,0:T(8,128)(2,1)S(1)}, u32[]{:S(2)}, u32[]{:S(2)}) collective-permute-start(bf16[4,2,64,384]{3,2,1,0:T(8,128)(2,1)S(1)} %get-tuple-element.49), channel_id=1, source_target_pairs={{0,5},{1,4},{2,7},{3,6},{4,1},{5,0},{6,3},{7,2},{8,13},{9,12},{10,... | collective-permute-start | bytes 1179656 | tf_op jit(solution)/shard_map/ppermute | solution.py:129
  118.3 2.6 %collective-permute-done.10.refs_2_ = bf16[4,2,64,384]{3,2,1,0:T(8,128)(2,1)S(1)} collective-permute-done((bf16[4,2,64,384]{3,2,1,0:T(8,128)(2,1)S(1)}, bf16[4,2,64,384]{3,2,1,0:T(8,128)(2,1)S(1)}, u32[]{:S(2)}, u32[]{:S(2)}) %collective-permute-start.10) | collective-permute-done | bytes 393248 | tf_op jit(solution)/shard_map/ppermute | solution.py:129
  120.9 4.4 %collective-permute-start.15 = (bf16[4,2,64,384]{3,2,1,0:T(8,128)(2,1)S(1)}, bf16[4,2,64,384]{3,2,1,0:T(8,128)(2,1)S(1)}, u32[]{:S(2)}, u32[]{:S(2)}) collective-permute-start(bf16[4,2,64,384]{3,2,1,0:T(8,128)(2,1)S(1)} %get-tuple-element.51), channel_id=1, source_target_pairs={{0,3},{1,2},{2,5},{3,4},{4,7},{5,6},{6,1},{7,0},{8,11},{9,10},{10,... | collective-permute-start | bytes 1179656 | tf_op jit(solution)/shard_map/ppermute | solution.py:129
  125.4 4.4 %collective-permute-done.11.refs_3_ = bf16[4,2,64,384]{3,2,1,0:T(8,128)(2,1)S(1)} collective-permute-done((bf16[4,2,64,384]{3,2,1,0:T(8,128)(2,1)S(1)}, bf16[4,2,64,384]{3,2,1,0:T(8,128)(2,1)S(1)}, u32[]{:S(2)}, u32[]{:S(2)}) %collective-permute-start.11) | collective-permute-done | bytes 393248 | tf_op jit(solution)/shard_map/ppermute | solution.py:129
  129.7 44.7 %collective-permute-done.12.refs_4_ = bf16[4,2,64,384]{3,2,1,0:T(8,128)(2,1)S(1)} collective-permute-done((bf16[4,2,64,384]{3,2,1,0:T(8,128)(2,1)S(1)}, bf16[4,2,64,384]{3,2,1,0:T(8,128)(2,1)S(1)}, u32[]{:S(2)}, u32[]{:S(2)}) %collective-permute-start.12) | collective-permute-done | bytes 393248 | tf_op jit(solution)/shard_map/ppermute | solution.py:129
  174.4 8.6 %collective-permute-done.13.refs_5_ = bf16[4,2,64,384]{3,2,1,0:T(8,128)(2,1)S(1)} collective-permute-done((bf16[4,2,64,384]{3,2,1,0:T(8,128)(2,1)S(1)}, bf16[4,2,64,384]{3,2,1,0:T(8,128)(2,1)S(1)}, u32[]{:S(2)}, u32[]{:S(2)}) %collective-permute-start.13) | collective-permute-done | bytes 393248 | tf_op jit(solution)/shard_map/ppermute | solution.py:129
  183.0 5.6 %collective-permute-done.15.refs_7_ = bf16[4,2,64,384]{3,2,1,0:T(8,128)(2,1)S(1)} collective-permute-done((bf16[4,2,64,384]{3,2,1,0:T(8,128)(2,1)S(1)}, bf16[4,2,64,384]{3,2,1,0:T(8,128)(2,1)S(1)}, u32[]{:S(2)}, u32[]{:S(2)}) %collective-permute-start.15) | collective-permute-done | bytes 393248 | tf_op jit(solution)/shard_map/ppermute | solution.py:129
  189.3 3.6 %unpack.1 = (bf16[1,2,64,3072]{3,2,1,0:T(8,128)(2,1)}, bf16[3,1,2,64,3072]{4,3,2,1,0:T(8,128)(2,1)}) custom-call(bf16[4,2,64,384]{3,2,1,0:T(8,128)(2,1)} %copy-done.4, bf16[4,2,64,384]{3,2,1,0:T(8,128)(2,1)} %copy-done.7, bf16[4,2,64,384]{3,2,1,0:T(8,128)(2,1)} %copy-done.8, bf16[4,2,64,384]{3,2,1,0:T(8,128)(2,1)} %copy-done.9, ...), custom_call_target="tpu_custom_call" | custom-call | tf_op jit(solution)/shard_map/unpack/pallas_call | solution.py:310
  (44 shorter events, 4.7 us)
Async XLA Ops:
  0.6 42.7 %copy-start.14 = (s32[32,2]{0,1:T(2,128)S(1)}, s32[32,2]{0,1:T(2,128)}, u32[]{:S(2)}) copy-start(s32[32,2]{0,1:T(2,128)} %param.11) | copy-start | bytes 772
  0.6 43.4 %copy-start.15 = (s32[32,2]{0,1:T(2,128)S(1)}, s32[32,2]{0,1:T(2,128)}, u32[]{:S(2)}) copy-start(s32[32,2]{0,1:T(2,128)} %param.12) | copy-start | bytes 772
  0.7 44.1 %copy-start.16 = (s32[32,2]{0,1:T(2,128)S(1)}, s32[32,2]{0,1:T(2,128)}, u32[]{:S(2)}) copy-start(s32[32,2]{0,1:T(2,128)} %param.13) | copy-start | bytes 772
  3.6 13.0 %collective-permute-start.2 = (bf16[4,2,64,384]{3,2,1,0:T(8,128)(2,1)}, bf16[4,2,64,384]{3,2,1,0:T(8,128)(2,1)S(1)}, u32[]{:S(2)}, u32[]{:S(2)}) collective-permute-start(bf16[4,2,64,384]{3,2,1,0:T(8,128)(2,1)} %get-tuple-element.33), channel_id=1, source_target_pairs={{0,1},{1,0},{2,3},{3,2},{4,5},{5,4},{6,7},{7,6},{8,9},{9,8},{10,11... | collective-permute-start | bytes 1179656 | tf_op jit(solution)/shard_map/ppermute | solution.py:129
  4.3 35.1 %collective-permute-start.3 = (bf16[4,2,64,384]{3,2,1,0:T(8,128)(2,1)}, bf16[4,2,64,384]{3,2,1,0:T(8,128)(2,1)S(1)}, u32[]{:S(2)}, u32[]{:S(2)}) collective-permute-start(bf16[4,2,64,384]{3,2,1,0:T(8,128)(2,1)} %get-tuple-element.34), channel_id=1, source_target_pairs={{0,2},{1,3},{2,4},{3,5},{4,6},{5,7},{6,0},{7,1},{8,10},{9,11},{10,... | collective-permute-start | bytes 1179656 | tf_op jit(solution)/shard_map/ppermute | solution.py:129
  7.3 55.5 %collective-permute-start.4 = (bf16[4,2,64,384]{3,2,1,0:T(8,128)(2,1)}, bf16[4,2,64,384]{3,2,1,0:T(8,128)(2,1)S(1)}, u32[]{:S(2)}, u32[]{:S(2)}) collective-permute-start(bf16[4,2,64,384]{3,2,1,0:T(8,128)(2,1)} %get-tuple-element.35), channel_id=1, source_target_pairs={{0,3},{1,2},{2,5},{3,4},{4,7},{5,6},{6,1},{7,0},{8,11},{9,10},{10,... | collective-permute-start | bytes 1179656 | tf_op jit(solution)/shard_map/ppermute | solution.py:129
  10.9 52.0 %collective-permute-start.5 = (bf16[4,2,64,384]{3,2,1,0:T(8,128)(2,1)}, bf16[4,2,64,384]{3,2,1,0:T(8,128)(2,1)S(1)}, u32[]{:S(2)}, u32[]{:S(2)}) collective-permute-start(bf16[4,2,64,384]{3,2,1,0:T(8,128)(2,1)} %get-tuple-element.36), channel_id=1, source_target_pairs={{0,4},{1,5},{2,6},{3,7},{4,0},{5,1},{6,2},{7,3},{8,12},{9,13},{10,... | collective-permute-start | bytes 1179656 | tf_op jit(solution)/shard_map/ppermute | solution.py:129
  11.6 51.2 %collective-permute-start.6 = (bf16[4,2,64,384]{3,2,1,0:T(8,128)(2,1)}, bf16[4,2,64,384]{3,2,1,0:T(8,128)(2,1)S(1)}, u32[]{:S(2)}, u32[]{:S(2)}) collective-permute-start(bf16[4,2,64,384]{3,2,1,0:T(8,128)(2,1)} %get-tuple-element.37), channel_id=1, source_target_pairs={{0,5},{1,4},{2,7},{3,6},{4,1},{5,0},{6,3},{7,2},{8,13},{9,12},{10,... | collective-permute-start | bytes 1179656 | tf_op jit(solution)/shard_map/ppermute | solution.py:129
  16.6 46.3 %collective-permute-start.7 = (bf16[4,2,64,384]{3,2,1,0:T(8,128)(2,1)}, bf16[4,2,64,384]{3,2,1,0:T(8,128)(2,1)S(1)}, u32[]{:S(2)}, u32[]{:S(2)}) collective-permute-start(bf16[4,2,64,384]{3,2,1,0:T(8,128)(2,1)} %get-tuple-element.38), channel_id=1, source_target_pairs={{0,6},{1,7},{2,0},{3,1},{4,2},{5,3},{6,4},{7,5},{8,14},{9,15},{10,... | collective-permute-start | bytes 1179656 | tf_op jit(solution)/shard_map/ppermute | solution.py:129
  39.4 25.9 %collective-permute-start.8 = (bf16[4,2,64,384]{3,2,1,0:T(8,128)(2,1)}, bf16[4,2,64,384]{3,2,1,0:T(8,128)(2,1)S(1)}, u32[]{:S(2)}, u32[]{:S(2)}) collective-permute-start(bf16[4,2,64,384]{3,2,1,0:T(8,128)(2,1)} %get-tuple-element.39), channel_id=1, source_target_pairs={{0,7},{1,6},{2,1},{3,0},{4,3},{5,2},{6,5},{7,4},{8,15},{9,14},{10,... | collective-permute-start | bytes 1179656 | tf_op jit(solution)/shard_map/ppermute | solution.py:129
  65.3 36.3 %copy-start.2 = (bf16[4,2,64,384]{3,2,1,0:T(8,128)(2,1)}, bf16[4,2,64,384]{3,2,1,0:T(8,128)(2,1)S(1)}, u32[]{:S(2)}) copy-start(bf16[4,2,64,384]{3,2,1,0:T(8,128)(2,1)S(1)} %collective-permute-done.8.refs_7_) | copy-start | bytes 1179652
  65.3 1.1 copy-start
  66.4 0.7 copy-start.5
  67.1 34.5 %copy-start.1 = (bf16[4,2,64,384]{3,2,1,0:T(8,128)(2,1)S(1)}, bf16[4,2,64,384]{3,2,1,0:T(8,128)(2,1)}, u32[]{:S(2)}) copy-start(bf16[4,2,64,384]{3,2,1,0:T(8,128)(2,1)} %get-tuple-element.32.refs_0_) | copy-start | bytes 1179652
  67.1 34.5 %copy-start.6 = (s32[10]{0:T(128)S(1)}, s32[10]{0:T(128)}, u32[]{:S(2)}) copy-start(s32[10]{0:T(128)} %plan.1) | copy-start | bytes 124
  70.6 0.9 copy-start.3
  71.5 29.3 %collective-permute-start = (bf16[512,384]{1,0:T(8,128)(2,1)}, bf16[512,384]{1,0:T(8,128)(2,1)S(1)}, u32[]{:S(2)}, u32[]{:S(2)}) collective-permute-start(bf16[512,384]{1,0:T(8,128)(2,1)} %param.1), channel_id=1, source_target_pairs={{0,8},{8,0},{16,24},{24,16},{32,40},{40,32},{48,56},{56,48},{64,72... | collective-permute-start | bytes 1179656 | tf_op jit(solution)/shard_map/cond/branch_1_fun/ppermute | solution.py:329
  106.4 0.8 copy-start.4
  107.1 10.9 %collective-permute-start.9 = (bf16[4,2,64,384]{3,2,1,0:T(8,128)(2,1)S(1)}, bf16[4,2,64,384]{3,2,1,0:T(8,128)(2,1)S(1)}, u32[]{:S(2)}, u32[]{:S(2)}) collective-permute-start(bf16[4,2,64,384]{3,2,1,0:T(8,128)(2,1)S(1)} %get-tuple-element.45), channel_id=1, source_target_pairs={{0,1},{1,0},{2,3},{3,2},{4,5},{5,4},{6,7},{7,6},{8,9},{9,8},{10,11... | collective-permute-start | bytes 1179656 | tf_op jit(solution)/shard_map/ppermute | solution.py:129
  108.1 12.9 %collective-permute-start.10 = (bf16[4,2,64,384]{3,2,1,0:T(8,128)(2,1)S(1)}, bf16[4,2,64,384]{3,2,1,0:T(8,128)(2,1)S(1)}, u32[]{:S(2)}, u32[]{:S(2)}) collective-permute-start(bf16[4,2,64,384]{3,2,1,0:T(8,128)(2,1)S(1)} %get-tuple-element.46), channel_id=1, source_target_pairs={{0,6},{1,7},{2,0},{3,1},{4,2},{5,3},{6,4},{7,5},{8,14},{9,15},{10,... | collective-permute-start | bytes 1179656 | tf_op jit(solution)/shard_map/ppermute | solution.py:129
  110.0 19.7 %collective-permute-start.11 = (bf16[4,2,64,384]{3,2,1,0:T(8,128)(2,1)S(1)}, bf16[4,2,64,384]{3,2,1,0:T(8,128)(2,1)S(1)}, u32[]{:S(2)}, u32[]{:S(2)}) collective-permute-start(bf16[4,2,64,384]{3,2,1,0:T(8,128)(2,1)S(1)} %get-tuple-element.47), channel_id=1, source_target_pairs={{0,7},{1,6},{2,1},{3,0},{4,3},{5,2},{6,5},{7,4},{8,15},{9,14},{10,... | collective-permute-start | bytes 1179656 | tf_op jit(solution)/shard_map/ppermute | solution.py:129
  112.3 62.1 %collective-permute-start.12 = (bf16[4,2,64,384]{3,2,1,0:T(8,128)(2,1)S(1)}, bf16[4,2,64,384]{3,2,1,0:T(8,128)(2,1)S(1)}, u32[]{:S(2)}, u32[]{:S(2)}) collective-permute-start(bf16[4,2,64,384]{3,2,1,0:T(8,128)(2,1)S(1)} %get-tuple-element.48), channel_id=1, source_target_pairs={{0,4},{1,5},{2,6},{3,7},{4,0},{5,1},{6,2},{7,3},{8,12},{9,13},{10,... | collective-permute-start | bytes 1179656 | tf_op jit(solution)/shard_map/ppermute | solution.py:129
  114.6 68.4 %collective-permute-start.13 = (bf16[4,2,64,384]{3,2,1,0:T(8,128)(2,1)S(1)}, bf16[4,2,64,384]{3,2,1,0:T(8,128)(2,1)S(1)}, u32[]{:S(2)}, u32[]{:S(2)}) collective-permute-start(bf16[4,2,64,384]{3,2,1,0:T(8,128)(2,1)S(1)} %get-tuple-element.49), channel_id=1, source_target_pairs={{0,5},{1,4},{2,7},{3,6},{4,1},{5,0},{6,3},{7,2},{8,13},{9,12},{10,... | collective-permute-start | bytes 1179656 | tf_op jit(solution)/shard_map/ppermute | solution.py:129
  118.1 70.5 %copy-start.7 = (bf16[4,2,64,384]{3,2,1,0:T(8,128)(2,1)}, bf16[4,2,64,384]{3,2,1,0:T(8,128)(2,1)S(1)}, u32[]{:S(2)}) copy-start(bf16[4,2,64,384]{3,2,1,0:T(8,128)(2,1)S(1)} %collective-permute-done.9.refs_1_) | copy-start | bytes 1179652
  118.1 64.9 %collective-permute-start.14 = (bf16[4,2,64,384]{3,2,1,0:T(8,128)(2,1)S(1)}, bf16[4,2,64,384]{3,2,1,0:T(8,128)(2,1)S(1)}, u32[]{:S(2)}, u32[]{:S(2)}) collective-permute-start(bf16[4,2,64,384]{3,2,1,0:T(8,128)(2,1)S(1)} %get-tuple-element.50), channel_id=1, source_target_pairs={{0,2},{1,3},{2,4},{3,5},{4,6},{5,7},{6,0},{7,1},{8,10},{9,11},{10,... | collective-permute-start | bytes 1179656 | tf_op jit(solution)/shard_map/ppermute | solution.py:129
  120.9 67.7 %copy-start.8 = (bf16[4,2,64,384]{3,2,1,0:T(8,128)(2,1)}, bf16[4,2,64,384]{3,2,1,0:T(8,128)(2,1)S(1)}, u32[]{:S(2)}) copy-start(bf16[4,2,64,384]{3,2,1,0:T(8,128)(2,1)S(1)} %collective-permute-done.10.refs_2_) | copy-start | bytes 1179652
  120.9 67.7 %collective-permute-start.15 = (bf16[4,2,64,384]{3,2,1,0:T(8,128)(2,1)S(1)}, bf16[4,2,64,384]{3,2,1,0:T(8,128)(2,1)S(1)}, u32[]{:S(2)}, u32[]{:S(2)}) collective-permute-start(bf16[4,2,64,384]{3,2,1,0:T(8,128)(2,1)S(1)} %get-tuple-element.51), channel_id=1, source_target_pairs={{0,3},{1,2},{2,5},{3,4},{4,7},{5,6},{6,1},{7,0},{8,11},{9,10},{10,... | collective-permute-start | bytes 1179656 | tf_op jit(solution)/shard_map/ppermute | solution.py:129
  129.7 58.9 %copy-start.9 = (bf16[4,2,64,384]{3,2,1,0:T(8,128)(2,1)}, bf16[4,2,64,384]{3,2,1,0:T(8,128)(2,1)S(1)}, u32[]{:S(2)}) copy-start(bf16[4,2,64,384]{3,2,1,0:T(8,128)(2,1)S(1)} %collective-permute-done.11.refs_3_) | copy-start | bytes 1179652
  174.4 14.2 %copy-start.10 = (bf16[4,2,64,384]{3,2,1,0:T(8,128)(2,1)}, bf16[4,2,64,384]{3,2,1,0:T(8,128)(2,1)S(1)}, u32[]{:S(2)}) copy-start(bf16[4,2,64,384]{3,2,1,0:T(8,128)(2,1)S(1)} %collective-permute-done.12.refs_4_) | copy-start | bytes 1179652
  183.0 5.6 %copy-start.11 = (bf16[4,2,64,384]{3,2,1,0:T(8,128)(2,1)}, bf16[4,2,64,384]{3,2,1,0:T(8,128)(2,1)S(1)}, u32[]{:S(2)}) copy-start(bf16[4,2,64,384]{3,2,1,0:T(8,128)(2,1)S(1)} %collective-permute-done.13.refs_5_) | copy-start | bytes 1179652
  183.0 5.6 %copy-start.12 = (bf16[4,2,64,384]{3,2,1,0:T(8,128)(2,1)}, bf16[4,2,64,384]{3,2,1,0:T(8,128)(2,1)S(1)}, u32[]{:S(2)}) copy-start(bf16[4,2,64,384]{3,2,1,0:T(8,128)(2,1)S(1)} %collective-permute-done.14.refs_6_) | copy-start | bytes 1179652
  188.6 0.8 copy-start.13
where the time goes:
time: 194 us; the launch traced here: 193 us
  waiting for transfers between devices  113 us (58%)
  starting transfers between devices  52.7 us (27%)
  Pallas kernels  16.8 us (9%)
  local copies, waits for them, and re-layouts  8.35 us (4%)
  between operations  2.26 us (1%)
    ppermute x14, waiting for transfers between devices, exchange(): received[k] = lax.ppermute(parts[k], 'seq', pairs)  104 us
    ppermute x14, starting transfers between devices, exchange(): received[k] = lax.ppermute(parts[k], 'seq', pairs)  32.8 us
    ppermute x1, starting transfers between devices, swap(): lax.ppermute(gift, 'dp', pairs)  20 us
    ppermute x1, waiting for transfers between devices, swap(): lax.ppermute(gift, 'dp', pairs)  9.37 us
    unnamed x37, local copies, waits for them, and re-layouts  6.25 us
    pallas_call x1, Pallas kernels, backward(): pl.pallas_call(backward_kernel, out_shape=[jax.ShapeDtypeStruct(parts[0]....  4.8 us
  transfers between devices with their start and end apart: 15, of which 9 were waited for; matrix products, arithmetic and copies ran while one was open for 2% of the time, Pallas kernels for 1%

commit v1 on v0

--- a/solution.py
+++ b/solution.py
@@ -13,7 +13,7 @@
 NEGATIVE = -1e30
 LOG2E = 1.4426950408889634
 CORES = 2
-ORDER = (4, 5, 2, 6, 3, 7, 1)
+ORDER = (4, 6, 5, 7, 2, 3, 1)
 CHUNKS = ((0, 3),)
 ANY = pl.BlockSpec(memory_space=pl.ANY)
 VMEM = pl.BlockSpec(memory_space=pltpu.VMEM)
@@ -65,14 +65,15 @@
     )(lengths, to_group, to_slot)
 
 
-def reached(seq, k, sign):
+def reached(group, seq, k, sign):
+    sign = sign * (1 - 2 * (group % 2))
     chips = SEQ // CORES
     chip = (seq // CORES + sign * (k // CORES) + chips) % chips
     return chip * CORES + (seq + k) % CORES
 
 
 def block_columns(k, device_width, chunk):
-    other = reached(lax.axis_index("seq"), k, 1)
+    other = reached(lax.axis_index("dp"), lax.axis_index("seq"), k, 1)
     start = pl.multiple_of(other * device_width + chunk[0] * HEAD, HEAD)
     return pl.ds(start, chunk[1] * HEAD)
 
@@ -125,17 +126,29 @@
 def exchange(parts, sign):
     received = list(parts)
     for k in ORDER:
-        pairs = [(i, reached(i, k, sign)) for i in range(SEQ)]
-        received[k] = lax.ppermute(parts[k], "seq", pairs)
+        pairs = [
+            (group * SEQ + i, group * SEQ + reached(group, i, k, sign))
+            for group in range(lax.axis_size("dp"))
+            for i in range(SEQ)
+        ]
+        received[k] = lax.ppermute(parts[k], ("dp", "seq"), pairs)
     return received
+
+
+def place_blocks():
+    group, seq = lax.axis_index("dp"), lax.axis_index("seq")
+    return [reached(group, seq, k, -1) for k in range(SEQ)]
+
+
+def block_rows(rows):
+    return [pl.ds(pl.multiple_of(block * rows, rows), rows) for block in place_blocks()]
 
 
 def token_numbers(shape, axis):
     rows = shape[axis] // SEQ
-    blocks = [reached(lax.axis_index("seq"), k, -1) for k in range(SEQ)]
     piece = shape[:axis] + (rows,) + shape[axis + 1 :]
     within = lax.broadcasted_iota(jnp.int32, piece, axis)
-    return jnp.concatenate([within + block * rows for block in blocks], axis=axis)
+    return jnp.concatenate([within + block * rows for block in place_blocks()], axis=axis)
 
 
 def head_columns(head):
@@ -152,9 +165,12 @@
     )
 
 
-def scores_of(queries, keys, valid_keys):
-    scores = dot(keys, queries, 1, 1) * (HEAD**-0.5 * LOG2E)
-    return jnp.where(valid_keys, scores, NEGATIVE)
+def scores_of(queries, keys, key_mask):
+    return dot(keys, queries, 1, 1) * (HEAD**-0.5 * LOG2E) + key_mask
+
+
+def mask_of_keys(tokens, count):
+    return jnp.where(token_numbers((tokens, 1), 0) < count, 0.0, NEGATIVE)
 
 
 def forward_kernel(plan, *refs):
@@ -171,21 +187,20 @@
 
         @pl.when(count > 0)
         def _():
-            valid_keys = token_numbers((tokens, tokens), 0) < count
+            key_mask = mask_of_keys(tokens, count)
             valid_queries = token_numbers((tokens, HEAD), 0) < count
             for head in range(heads):
                 columns = head_columns(head)
                 queries, keys, values = (gathered(parts, n, slot, columns) for n in range(3))
-                scores = scores_of(queries, keys, valid_keys)
+                scores = scores_of(queries, keys, key_mask)
                 largest = jnp.max(scores, axis=0, keepdims=True)
                 exponent = jnp.exp2(scores - largest)
-                inverse = 1.0 / jnp.sum(exponent, axis=0, keepdims=True)
-                weights = (exponent * inverse).astype(jnp.bfloat16)
+                total = jnp.sum(exponent, axis=0, keepdims=True)
+                weights = (exponent * (1.0 / total)).astype(jnp.bfloat16)
                 output = dot(values, weights, 0, 0).T
                 output = jnp.where(valid_queries, output, 0.0).astype(jnp.bfloat16)
                 out[slot, :, columns] = output
-                stats[slot, 2 * head : 2 * head + 1, :] = largest
-                stats[slot, 2 * head + 1 : 2 * head + 2, :] = inverse
+                stats[slot, head : head + 1, :] = largest + jnp.log2(total)
 
     for number, gift in enumerate(gifts):
         for slot in range(slots):
@@ -193,12 +208,13 @@
 
             @pl.when((plan[2 * number] == 1) & chosen)
             def _():
-                gift[...] = out[slot]
+                for k, held in enumerate(block_rows(rows)):
+                    gift[held] = out[slot, k * rows : (k + 1) * rows]
 
             @pl.when((plan[2 * number] == 2) & chosen)
             def _():
-                for k, part in enumerate(parts):
-                    gift[k * rows : (k + 1) * rows] = part[3, slot]
+                for held, part in zip(block_rows(rows), parts):
+                    gift[held] = part[3, slot]
 
 
 def forward(plan, parts):
@@ -227,12 +243,18 @@
     heads = width // HEAD
     for slot in range(slots):
         count = plan[8 + slot]
-        for choice, source in ((0, home_out.at[slot]), (1, even), (2, odd)):
+
+        @pl.when(plan[6 + slot] == 0)
+        def _():
+            for k, out in enumerate(outs):
+                out[0, slot] = home_out[slot, k * rows : (k + 1) * rows]
+
+        for choice, source in ((1, even), (2, odd)):
 
             @pl.when(plan[6 + slot] == choice)
             def _():
-                for k, out in enumerate(outs):
-                    out[0, slot] = source[k * rows : (k + 1) * rows]
+                for held, out in zip(block_rows(rows), outs):
+                    out[0, slot] = source[held]
 
         @pl.when(plan[6 + slot] == 3)
         def _():
@@ -248,7 +270,7 @@
         @pl.when(count > 0)
         def _():
             source = plan[4 + slot]
-            valid_keys = token_numbers((tokens, tokens), 0) < count
+            key_mask = mask_of_keys(tokens, count)
             valid_queries = token_numbers((tokens, HEAD), 0) < count
             factor = HEAD**-0.5
             for head in range(heads):
@@ -256,13 +278,15 @@
                 queries, keys, values, own = (
                     gathered(parts, n, slot, columns) for n in range(ARRAYS)
                 )
-                moved = jnp.where(source == 1, even[:, columns], odd[:, columns])
+                moved = [
+                    jnp.where(source == 1, even[held, columns], odd[held, columns])
+                    for held in block_rows(rows)
+                ]
+                moved = jnp.concatenate(moved, axis=0)
                 upstream = jnp.where(source == 0, own, moved)
                 upstream = jnp.where(valid_queries, upstream, jnp.zeros_like(upstream))
-                scores = scores_of(queries, keys, valid_keys)
-                largest = stats[slot, 2 * head : 2 * head + 1, :]
-                inverse = stats[slot, 2 * head + 1 : 2 * head + 2, :]
-                weights = jnp.exp2(scores - largest) * inverse
+                scores = scores_of(queries, keys, key_mask)
+                weights = jnp.exp2(scores - stats[slot, head : head + 1, :])
                 grad_values = dot(weights.astype(jnp.bfloat16), upstream, 1, 0)
                 grad_weights = dot(values, upstream, 1, 1)
                 inner = jnp.sum(grad_weights * weights, axis=0, keepdims=True)
@@ -286,11 +310,11 @@
     )(plan, *parts, home_out, stats, even, odd)
 
 
-def unpack_kernel(chunk, *refs):
-    parts, (attended, grads, sem) = refs[:SEQ], refs[-3:]
+def unpack_kernel(chunk, steps, *refs):
+    parts, (attended, grads, sem) = refs[: len(steps)], refs[-3:]
     device_width = grads.shape[-1] // SEQ
     copies = []
-    for k, part in enumerate(parts):
+    for k, part in zip(steps, parts):
         columns = block_columns(k, device_width, chunk)
         copies += [
             pltpu.make_async_copy(part.at[0], attended.at[0, :, :, columns], sem.at[k, 0]),
@@ -304,18 +328,19 @@
         copy.wait()
 
 
-def unpack(parts, chunk, device_heads, filled=()):
+def unpack(parts, steps, chunk, device_heads, filled=()):
+    parts = [parts[k] for k in steps]
     _, slots, rows, _ = parts[0].shape
     features = device_heads * HEAD * SEQ
     return pl.pallas_call(
-        functools.partial(unpack_kernel, chunk),
+        functools.partial(unpack_kernel, chunk, steps),
         out_shape=[
             jax.ShapeDtypeStruct((1, slots, rows, features), jnp.bfloat16),
             jax.ShapeDtypeStruct((3, 1, slots, rows, features), jnp.bfloat16),
         ],
-        in_specs=[VMEM] * SEQ + [ANY] * len(filled),
+        in_specs=[VMEM] * len(steps) + [ANY] * len(filled),
         out_specs=[ANY, ANY],
-        input_output_aliases={SEQ + n: n for n in range(len(filled))},
+        input_output_aliases={len(steps) + n: n for n in range(len(filled))},
         scratch_shapes=[pltpu.SemaphoreType.DMA((SEQ, 2))],
         name="unpack",
     )(*parts, *filled)
@@ -347,7 +372,8 @@
         returned.append(exchange(backward(plan, parts, home_out, stats, even, odd), -1))
     results = ()
     for parts, chunk in zip(returned, CHUNKS):
-        results = unpack(parts, chunk, device_heads, results)
+        for steps in ((0, *ORDER[:4]), ORDER[4:]):
+            results = unpack(parts, steps, chunk, device_heads, results)
     return tuple(results)
 
 

time: 194 us -> 188 us (0.969)
  the two profiles are of different devices: /device:TPU:33 before, /device:TPU:31 now
where the time goes in v1:
time: 188 us; the launch traced here: 184 us
  waiting for transfers between devices  97.9 us (52%)
  starting transfers between devices  55.8 us (30%)
  Pallas kernels  19.3 us (10%)
  local copies, waits for them, and re-layouts  9.14 us (5%)
  between operations  2.16 us (1%)
    ppermute x14, waiting for transfers between devices, exchange(): received[k] = lax.ppermute(parts[k], ('dp', 'seq'), pairs)  88.3 us
    ppermute x14, starting transfers between devices, exchange(): received[k] = lax.ppermute(parts[k], ('dp', 'seq'), pairs)  35.6 us
    ppermute x1, starting transfers between devices, swap(): lax.ppermute(gift, 'dp', pairs)  20.2 us
    ppermute x1, waiting for transfers between devices, swap(): lax.ppermute(gift, 'dp', pairs)  9.58 us
    unnamed x37, local copies, waits for them, and re-layouts  7.14 us
    pallas_call x1, Pallas kernels, backward(): pl.pallas_call(backward_kernel, out_shape=[jax.ShapeDtypeStruct(parts[0]....  5.72 us
    pallas_call x2, Pallas kernels, unpack(): pl.pallas_call(functools.partial(unpack_kernel, chunk, steps), out_shape=...  5.25 us
  transfers between devices with their start and end apart: 15, of which 12 were waited for; matrix products, arithmetic and copies ran while one was open for 2% of the time, Pallas kernels for 3%

profile of v1, /device:TPU:31, one launch (start us, length us, event | category | flops | bytes accessed | tf_op | source)
XLA Modules:
  0.0 184.3 jit_solution(3329210309511158267)
XLA Ops:
  0.7 2.9 %pack.1 = (bf16[4,2,64,384]{3,2,1,0:T(8,128)(2,1)}, bf16[4,2,64,384]{3,2,1,0:T(8,128)(2,1)}, bf16[4,2,64,384]{3,2,1,0:T(8,128)(2,1)}, bf16[4,2,64,384]{3,2,1,0:T...) custom-call(bf16[3,1,2,64,3072]{4,3,2,1,0:T(8,128)(2,1)} %qkv.1, ...), custom_call_target="tpu_custom_call" | custom-call | tf_op jit(solution)/shard_map/pack/pallas_call | solution.py:112
  4.3 3.0 %collective-permute-start.3 = (bf16[4,2,64,384]{3,2,1,0:T(8,128)(2,1)}, bf16[4,2,64,384]{3,2,1,0:T(8,128)(2,1)S(1)}, u32[]{:S(2)}, u32[]{:S(2)}) collective-permute-start(bf16[4,2,64,384]{3,2,1,0:T(8,128)(2,1)} %get-tuple-element.36), channel_id=1, source_target_pairs={{0,2},{1,3},{2,4},{3,5},{4,6},{5,7},{6,0},{7,1},{8,14},{9,15},{10,... | collective-permute-start | bytes 1179656 | tf_op jit(solution)/shard_map/ppermute | solution.py:134
  7.3 4.4 %collective-permute-start.4 = (bf16[4,2,64,384]{3,2,1,0:T(8,128)(2,1)}, bf16[4,2,64,384]{3,2,1,0:T(8,128)(2,1)S(1)}, u32[]{:S(2)}, u32[]{:S(2)}) collective-permute-start(bf16[4,2,64,384]{3,2,1,0:T(8,128)(2,1)} %get-tuple-element.37), channel_id=1, source_target_pairs={{0,3},{1,2},{2,5},{3,4},{4,7},{5,6},{6,1},{7,0},{8,15},{9,14},{10,... | collective-permute-start | bytes 1179656 | tf_op jit(solution)/shard_map/ppermute | solution.py:134
  12.5 5.0 %collective-permute-start.6 = (bf16[4,2,64,384]{3,2,1,0:T(8,128)(2,1)}, bf16[4,2,64,384]{3,2,1,0:T(8,128)(2,1)S(1)}, u32[]{:S(2)}, u32[]{:S(2)}) collective-permute-start(bf16[4,2,64,384]{3,2,1,0:T(8,128)(2,1)} %get-tuple-element.39), channel_id=1, source_target_pairs={{0,5},{1,4},{2,7},{3,6},{4,1},{5,0},{6,3},{7,2},{8,13},{9,12},{10,... | collective-permute-start | bytes 1179656 | tf_op jit(solution)/shard_map/ppermute | solution.py:134
  17.5 2.5 %collective-permute-done.3.refs_2_ = bf16[4,2,64,384]{3,2,1,0:T(8,128)(2,1)S(1)} collective-permute-done((bf16[4,2,64,384]{3,2,1,0:T(8,128)(2,1)}, bf16[4,2,64,384]{3,2,1,0:T(8,128)(2,1)S(1)}, u32[]{:S(2)}, u32[]{:S(2)}) %collective-permute-start.3) | collective-permute-done | bytes 393248 | tf_op jit(solution)/shard_map/ppermute | solution.py:134
  19.9 3.5 %collective-permute-start.8 = (bf16[4,2,64,384]{3,2,1,0:T(8,128)(2,1)}, bf16[4,2,64,384]{3,2,1,0:T(8,128)(2,1)S(1)}, u32[]{:S(2)}, u32[]{:S(2)}) collective-permute-start(bf16[4,2,64,384]{3,2,1,0:T(8,128)(2,1)} %get-tuple-element.41), channel_id=1, source_target_pairs={{0,7},{1,6},{2,1},{3,0},{4,3},{5,2},{6,5},{7,4},{8,11},{9,10},{10,... | collective-permute-start | bytes 1179656 | tf_op jit(solution)/shard_map/ppermute | solution.py:134
  25.5 2.0 %plan.1 = s32[10]{0:T(128)} custom-call(s32[32,2]{1,0:T(8,128)} %copy.9.lengths, s32[32,2]{1,0:T(8,128)} %copy.10.to_group, s32[32,2]{1,0:T(8,128)} %copy.11.to_slot), custom_call_target="tpu_custom_call" | custom-call | tf_op jit(solution)/shard_map/plan/pallas_call | solution.py:59
  27.5 1.3 fusion
  30.1 9.1 %collective-permute-done.5.refs_4_ = bf16[4,2,64,384]{3,2,1,0:T(8,128)(2,1)S(1)} collective-permute-done((bf16[4,2,64,384]{3,2,1,0:T(8,128)(2,1)}, bf16[4,2,64,384]{3,2,1,0:T(8,128)(2,1)S(1)}, u32[]{:S(2)}, u32[]{:S(2)}) %collective-permute-start.5) | collective-permute-done | bytes 393248 | tf_op jit(solution)/shard_map/ppermute | solution.py:134
  39.2 8.8 %collective-permute-done.6.refs_5_ = bf16[4,2,64,384]{3,2,1,0:T(8,128)(2,1)S(1)} collective-permute-done((bf16[4,2,64,384]{3,2,1,0:T(8,128)(2,1)}, bf16[4,2,64,384]{3,2,1,0:T(8,128)(2,1)S(1)}, u32[]{:S(2)}, u32[]{:S(2)}) %collective-permute-start.6) | collective-permute-done | bytes 393248 | tf_op jit(solution)/shard_map/ppermute | solution.py:134
  48.0 6.1 %collective-permute-done.7.refs_6_ = bf16[4,2,64,384]{3,2,1,0:T(8,128)(2,1)S(1)} collective-permute-done((bf16[4,2,64,384]{3,2,1,0:T(8,128)(2,1)}, bf16[4,2,64,384]{3,2,1,0:T(8,128)(2,1)S(1)}, u32[]{:S(2)}, u32[]{:S(2)}) %collective-permute-start.7) | collective-permute-done | bytes 393248 | tf_op jit(solution)/shard_map/ppermute | solution.py:134
  54.1 8.4 %collective-permute-done.8.refs_7_ = bf16[4,2,64,384]{3,2,1,0:T(8,128)(2,1)S(1)} collective-permute-done((bf16[4,2,64,384]{3,2,1,0:T(8,128)(2,1)}, bf16[4,2,64,384]{3,2,1,0:T(8,128)(2,1)S(1)}, u32[]{:S(2)}, u32[]{:S(2)}) %collective-permute-start.8) | collective-permute-done | bytes 393248 | tf_op jit(solution)/shard_map/ppermute | solution.py:134
  62.6 1.1 copy-done
  64.3 3.5 %forward.1 = (bf16[2,512,384]{2,1,0:T(8,128)(2,1)S(1)}, f32[2,8,512]{2,1,0:T(8,128)S(1)}, bf16[512,384]{1,0:T(8,128)(2,1)}, bf16[512,384]{1,0:T(8,128)(2,1)}) custom-call(s32[10]{0:T(128)S(1)} %copy-done.5, bf16[4,2,64,384]{3,2,1,0:T(8,128)(2,1)S(1)} %copy-done, bf16[4,2,64,384]{3,2,1,0:T(8,128)(2,1)S(1)} %collective-permute-done.2.refs_1_, ...), custom_call_target="tpu_custom_call" | custom-call | tf_op jit(solution)/shard_map/forward/pallas_call | solution.py:224
  67.8 0.9 copy-done.3
  68.7 30.5 %conditional.2 = (bf16[512,384]{1,0:T(8,128)(2,1)}) conditional(s32[]{:T(128)} %bitcast, bf16[512,384]{1,0:T(8,128)(2,1)} %get-tuple-element.44, bf16[512,384]{1,0:T(8,128)(2,1)} %get-tuple-element.44), branch_computations={%region_0.0_spmd, %region_1.0_spmd} | conditional | bytes 2359344 | solution.py:353
  68.7 20.2 %collective-permute-start = (bf16[512,384]{1,0:T(8,128)(2,1)}, bf16[512,384]{1,0:T(8,128)(2,1)S(1)}, u32[]{:S(2)}, u32[]{:S(2)}) collective-permute-start(bf16[512,384]{1,0:T(8,128)(2,1)} %param.1), channel_id=1, source_target_pairs={{0,8},{8,0},{16,24},{24,16},{32,40},{40,32},{48,56},{56,48},{64,72... | collective-permute-start | bytes 1179656 | tf_op jit(solution)/shard_map/cond/branch_1_fun/ppermute | solution.py:354
  88.8 9.6 %collective-permute-done = bf16[512,384]{1,0:T(8,128)(2,1)S(1)} collective-permute-done((bf16[512,384]{1,0:T(8,128)(2,1)}, bf16[512,384]{1,0:T(8,128)(2,1)S(1)}, u32[]{:S(2)}, u32[]{:S(2)}) %collective-permute-start) | collective-permute-done | bytes 393248 | tf_op jit(solution)/shard_map/cond/branch_1_fun/ppermute | solution.py:354
  99.2 5.7 %backward.1 = (bf16[4,2,64,384]{3,2,1,0:T(8,128)(2,1)S(1)}, bf16[4,2,64,384]{3,2,1,0:T(8,128)(2,1)S(1)}, bf16[4,2,64,384]{3,2,1,0:T(8,128)(2,1)}, bf16[4,2,64,38...) custom-call(s32[10]{0:T(128)S(1)} %copy-done.6, ...), custom_call_target="tpu_custom_call" | custom-call | tf_op jit(solution)/shard_map/backward/pallas_call | solution.py:303
  105.6 4.1 %collective-permute-start.12 = (bf16[4,2,64,384]{3,2,1,0:T(8,128)(2,1)S(1)}, bf16[4,2,64,384]{3,2,1,0:T(8,128)(2,1)S(1)}, u32[]{:S(2)}, u32[]{:S(2)}) collective-permute-start(bf16[4,2,64,384]{3,2,1,0:T(8,128)(2,1)S(1)} %get-tuple-element.50), channel_id=1, source_target_pairs={{0,4},{1,5},{2,6},{3,7},{4,0},{5,1},{6,2},{7,3},{8,12},{9,13},{10,... | collective-permute-start | bytes 1179656 | tf_op jit(solution)/shard_map/ppermute | solution.py:134
  109.8 3.6 %collective-permute-start.9 = (bf16[4,2,64,384]{3,2,1,0:T(8,128)(2,1)}, bf16[4,2,64,384]{3,2,1,0:T(8,128)(2,1)S(1)}, u32[]{:S(2)}, u32[]{:S(2)}) collective-permute-start(bf16[4,2,64,384]{3,2,1,0:T(8,128)(2,1)} %get-tuple-element.46), channel_id=1, source_target_pairs={{0,6},{1,7},{2,0},{3,1},{4,2},{5,3},{6,4},{7,5},{8,10},{9,11},{10,... | collective-permute-start | bytes 1179656 | tf_op jit(solution)/shard_map/ppermute | solution.py:134
  113.4 2.6 %collective-permute-start.14 = (bf16[4,2,64,384]{3,2,1,0:T(8,128)(2,1)S(1)}, bf16[4,2,64,384]{3,2,1,0:T(8,128)(2,1)S(1)}, u32[]{:S(2)}, u32[]{:S(2)}) collective-permute-start(bf16[4,2,64,384]{3,2,1,0:T(8,128)(2,1)S(1)} %get-tuple-element.52), channel_id=1, source_target_pairs={{0,5},{1,4},{2,7},{3,6},{4,1},{5,0},{6,3},{7,2},{8,13},{9,12},{10,... | collective-permute-start | bytes 1179656 | tf_op jit(solution)/shard_map/ppermute | solution.py:134
  116.0 11.4 %collective-permute-done.12.refs_1_ = bf16[4,2,64,384]{3,2,1,0:T(8,128)(2,1)S(1)} collective-permute-done((bf16[4,2,64,384]{3,2,1,0:T(8,128)(2,1)S(1)}, bf16[4,2,64,384]{3,2,1,0:T(8,128)(2,1)S(1)}, u32[]{:S(2)}, u32[]{:S(2)}) %collective-permute-start.12) | collective-permute-done | bytes 393248 | tf_op jit(solution)/shard_map/ppermute | solution.py:134
  127.4 5.6 %collective-permute-start.10 = (bf16[4,2,64,384]{3,2,1,0:T(8,128)(2,1)}, bf16[4,2,64,384]{3,2,1,0:T(8,128)(2,1)S(1)}, u32[]{:S(2)}, u32[]{:S(2)}) collective-permute-start(bf16[4,2,64,384]{3,2,1,0:T(8,128)(2,1)} %get-tuple-element.47), channel_id=1, source_target_pairs={{0,7},{1,6},{2,1},{3,0},{4,3},{5,2},{6,5},{7,4},{8,11},{9,10},{10,... | collective-permute-start | bytes 1179656 | tf_op jit(solution)/shard_map/ppermute | solution.py:134
  133.0 1.8 collective-permute-done.13.refs_2_
  134.8 2.2 %collective-permute-start.11 = (bf16[4,2,64,384]{3,2,1,0:T(8,128)(2,1)S(1)}, bf16[4,2,64,384]{3,2,1,0:T(8,128)(2,1)S(1)}, u32[]{:S(2)}, u32[]{:S(2)}) collective-permute-start(bf16[4,2,64,384]{3,2,1,0:T(8,128)(2,1)S(1)} %get-tuple-element.48), channel_id=1, source_target_pairs={{0,1},{1,0},{2,3},{3,2},{4,5},{5,4},{6,7},{7,6},{8,9},{9,8},{10,11... | collective-permute-start | bytes 1179656 | tf_op jit(solution)/shard_map/ppermute | solution.py:134
  137.0 17.9 %collective-permute-done.14.refs_3_ = bf16[4,2,64,384]{3,2,1,0:T(8,128)(2,1)S(1)} collective-permute-done((bf16[4,2,64,384]{3,2,1,0:T(8,128)(2,1)S(1)}, bf16[4,2,64,384]{3,2,1,0:T(8,128)(2,1)S(1)}, u32[]{:S(2)}, u32[]{:S(2)}) %collective-permute-start.14) | collective-permute-done | bytes 393248 | tf_op jit(solution)/shard_map/ppermute | solution.py:134
  155.0 4.9 %collective-permute-done.15.refs_4_ = bf16[4,2,64,384]{3,2,1,0:T(8,128)(2,1)S(1)} collective-permute-done((bf16[4,2,64,384]{3,2,1,0:T(8,128)(2,1)S(1)}, bf16[4,2,64,384]{3,2,1,0:T(8,128)(2,1)S(1)}, u32[]{:S(2)}, u32[]{:S(2)}) %collective-permute-start.15) | collective-permute-done | bytes 393248 | tf_op jit(solution)/shard_map/ppermute | solution.py:134
  160.6 2.9 %unpack.2 = (bf16[1,2,64,3072]{3,2,1,0:T(8,128)(2,1)}, bf16[3,1,2,64,3072]{4,3,2,1,0:T(8,128)(2,1)}) custom-call(bf16[4,2,64,384]{3,2,1,0:T(8,128)(2,1)} %copy-done.4, bf16[4,2,64,384]{3,2,1,0:T(8,128)(2,1)} %copy-done.10, bf16[4,2,64,384]{3,2,1,0:T(8,128)(2,1)} %copy-done.11, bf16[4,2,64,384]{3,2,1,0:T(8,128)(2,1)} %copy-done.12, ...), custom_call_target="tpu_custom_call" | custom-call | tf_op jit(solution)/shard_map/unpack/pallas_call | solution.py:335
  163.5 8.9 %collective-permute-done.9.refs_0_ = bf16[4,2,64,384]{3,2,1,0:T(8,128)(2,1)S(1)} collective-permute-done((bf16[4,2,64,384]{3,2,1,0:T(8,128)(2,1)}, bf16[4,2,64,384]{3,2,1,0:T(8,128)(2,1)S(1)}, u32[]{:S(2)}, u32[]{:S(2)}) %collective-permute-start.9) | collective-permute-done | bytes 393248 | tf_op jit(solution)/shard_map/ppermute | solution.py:134
  172.4 8.4 %collective-permute-done.10.refs_1_ = bf16[4,2,64,384]{3,2,1,0:T(8,128)(2,1)S(1)} collective-permute-done((bf16[4,2,64,384]{3,2,1,0:T(8,128)(2,1)}, bf16[4,2,64,384]{3,2,1,0:T(8,128)(2,1)S(1)}, u32[]{:S(2)}, u32[]{:S(2)}) %collective-permute-start.10) | collective-permute-done | bytes 393248 | tf_op jit(solution)/shard_map/ppermute | solution.py:134
  181.8 2.4 %unpack.3 = (bf16[1,2,64,3072]{3,2,1,0:T(8,128)(2,1)}, bf16[3,1,2,64,3072]{4,3,2,1,0:T(8,128)(2,1)}) custom-call(bf16[4,2,64,384]{3,2,1,0:T(8,128)(2,1)} %copy-done.7, bf16[4,2,64,384]{3,2,1,0:T(8,128)(2,1)} %copy-done.8, bf16[4,2,64,384]{3,2,1,0:T(8,128)(2,1)} %copy-done.9, ...), custom_call_target="tpu_custom_call", output_to_operand_aliasing={{0}: (3, {}), {1}: (4, {})} | custom-call | tf_op jit(solution)/shard_map/unpack/pallas_call | solution.py:335
  (45 shorter events, 7.4 us)
Async XLA Ops:
  0.6 22.8 %copy-start.14 = (s32[32,2]{0,1:T(2,128)S(1)}, s32[32,2]{0,1:T(2,128)}, u32[]{:S(2)}) copy-start(s32[32,2]{0,1:T(2,128)} %param.11) | copy-start | bytes 772
  0.6 23.5 %copy-start.15 = (s32[32,2]{0,1:T(2,128)S(1)}, s32[32,2]{0,1:T(2,128)}, u32[]{:S(2)}) copy-start(s32[32,2]{0,1:T(2,128)} %param.12) | copy-start | bytes 772
  0.7 24.2 %copy-start.16 = (s32[32,2]{0,1:T(2,128)S(1)}, s32[32,2]{0,1:T(2,128)}, u32[]{:S(2)}) copy-start(s32[32,2]{0,1:T(2,128)} %param.13) | copy-start | bytes 772
  3.5 13.9 %collective-permute-start.2 = (bf16[4,2,64,384]{3,2,1,0:T(8,128)(2,1)}, bf16[4,2,64,384]{3,2,1,0:T(8,128)(2,1)S(1)}, u32[]{:S(2)}, u32[]{:S(2)}) collective-permute-start(bf16[4,2,64,384]{3,2,1,0:T(8,128)(2,1)} %get-tuple-element.35), channel_id=1, source_target_pairs={{0,1},{1,0},{2,3},{3,2},{4,5},{5,4},{6,7},{7,6},{8,9},{9,8},{10,11... | collective-permute-start | bytes 1179656 | tf_op jit(solution)/shard_map/ppermute | solution.py:134
  4.3 15.6 %collective-permute-start.3 = (bf16[4,2,64,384]{3,2,1,0:T(8,128)(2,1)}, bf16[4,2,64,384]{3,2,1,0:T(8,128)(2,1)S(1)}, u32[]{:S(2)}, u32[]{:S(2)}) collective-permute-start(bf16[4,2,64,384]{3,2,1,0:T(8,128)(2,1)} %get-tuple-element.36), channel_id=1, source_target_pairs={{0,2},{1,3},{2,4},{3,5},{4,6},{5,7},{6,0},{7,1},{8,14},{9,15},{10,... | collective-permute-start | bytes 1179656 | tf_op jit(solution)/shard_map/ppermute | solution.py:134
  7.3 22.8 %collective-permute-start.4 = (bf16[4,2,64,384]{3,2,1,0:T(8,128)(2,1)}, bf16[4,2,64,384]{3,2,1,0:T(8,128)(2,1)S(1)}, u32[]{:S(2)}, u32[]{:S(2)}) collective-permute-start(bf16[4,2,64,384]{3,2,1,0:T(8,128)(2,1)} %get-tuple-element.37), channel_id=1, source_target_pairs={{0,3},{1,2},{2,5},{3,4},{4,7},{5,6},{6,1},{7,0},{8,15},{9,14},{10,... | collective-permute-start | bytes 1179656 | tf_op jit(solution)/shard_map/ppermute | solution.py:134
  11.8 27.4 %collective-permute-start.5 = (bf16[4,2,64,384]{3,2,1,0:T(8,128)(2,1)}, bf16[4,2,64,384]{3,2,1,0:T(8,128)(2,1)S(1)}, u32[]{:S(2)}, u32[]{:S(2)}) collective-permute-start(bf16[4,2,64,384]{3,2,1,0:T(8,128)(2,1)} %get-tuple-element.38), channel_id=1, source_target_pairs={{0,4},{1,5},{2,6},{3,7},{4,0},{5,1},{6,2},{7,3},{8,12},{9,13},{10,... | collective-permute-start | bytes 1179656 | tf_op jit(solution)/shard_map/ppermute | solution.py:134
  12.5 35.5 %collective-permute-start.6 = (bf16[4,2,64,384]{3,2,1,0:T(8,128)(2,1)}, bf16[4,2,64,384]{3,2,1,0:T(8,128)(2,1)S(1)}, u32[]{:S(2)}, u32[]{:S(2)}) collective-permute-start(bf16[4,2,64,384]{3,2,1,0:T(8,128)(2,1)} %get-tuple-element.39), channel_id=1, source_target_pairs={{0,5},{1,4},{2,7},{3,6},{4,1},{5,0},{6,3},{7,2},{8,13},{9,12},{10,... | collective-permute-start | bytes 1179656 | tf_op jit(solution)/shard_map/ppermute | solution.py:134
  17.5 36.7 %collective-permute-start.7 = (bf16[4,2,64,384]{3,2,1,0:T(8,128)(2,1)}, bf16[4,2,64,384]{3,2,1,0:T(8,128)(2,1)S(1)}, u32[]{:S(2)}, u32[]{:S(2)}) collective-permute-start(bf16[4,2,64,384]{3,2,1,0:T(8,128)(2,1)} %get-tuple-element.40), channel_id=1, source_target_pairs={{0,6},{1,7},{2,0},{3,1},{4,2},{5,3},{6,4},{7,5},{8,10},{9,11},{10,... | collective-permute-start | bytes 1179656 | tf_op jit(solution)/shard_map/ppermute | solution.py:134
  19.9 42.6 %collective-permute-start.8 = (bf16[4,2,64,384]{3,2,1,0:T(8,128)(2,1)}, bf16[4,2,64,384]{3,2,1,0:T(8,128)(2,1)S(1)}, u32[]{:S(2)}, u32[]{:S(2)}) collective-permute-start(bf16[4,2,64,384]{3,2,1,0:T(8,128)(2,1)} %get-tuple-element.41), channel_id=1, source_target_pairs={{0,7},{1,6},{2,1},{3,0},{4,3},{5,2},{6,5},{7,4},{8,11},{9,10},{10,... | collective-permute-start | bytes 1179656 | tf_op jit(solution)/shard_map/ppermute | solution.py:134
  62.6 36.6 %copy-start.2 = (bf16[4,2,64,384]{3,2,1,0:T(8,128)(2,1)}, bf16[4,2,64,384]{3,2,1,0:T(8,128)(2,1)S(1)}, u32[]{:S(2)}) copy-start(bf16[4,2,64,384]{3,2,1,0:T(8,128)(2,1)S(1)} %collective-permute-done.8.refs_7_) | copy-start | bytes 1179652
  62.6 1.1 copy-start
  63.7 0.6 copy-start.5
  64.3 34.9 %copy-start.1 = (bf16[4,2,64,384]{3,2,1,0:T(8,128)(2,1)S(1)}, bf16[4,2,64,384]{3,2,1,0:T(8,128)(2,1)}, u32[]{:S(2)}) copy-start(bf16[4,2,64,384]{3,2,1,0:T(8,128)(2,1)} %get-tuple-element.34.refs_0_) | copy-start | bytes 1179652
  64.3 34.9 %copy-start.6 = (s32[10]{0:T(128)S(1)}, s32[10]{0:T(128)}, u32[]{:S(2)}) copy-start(s32[10]{0:T(128)} %plan.1) | copy-start | bytes 124
  67.8 0.9 copy-start.3
  68.7 29.8 %collective-permute-start = (bf16[512,384]{1,0:T(8,128)(2,1)}, bf16[512,384]{1,0:T(8,128)(2,1)S(1)}, u32[]{:S(2)}, u32[]{:S(2)}) collective-permute-start(bf16[512,384]{1,0:T(8,128)(2,1)} %param.1), channel_id=1, source_target_pairs={{0,8},{8,0},{16,24},{24,16},{32,40},{40,32},{48,56},{56,48},{64,72... | collective-permute-start | bytes 1179656 | tf_op jit(solution)/shard_map/cond/branch_1_fun/ppermute | solution.py:354
  104.9 0.8 copy-start.4
  105.6 21.8 %collective-permute-start.12 = (bf16[4,2,64,384]{3,2,1,0:T(8,128)(2,1)S(1)}, bf16[4,2,64,384]{3,2,1,0:T(8,128)(2,1)S(1)}, u32[]{:S(2)}, u32[]{:S(2)}) collective-permute-start(bf16[4,2,64,384]{3,2,1,0:T(8,128)(2,1)S(1)} %get-tuple-element.50), channel_id=1, source_target_pairs={{0,4},{1,5},{2,6},{3,7},{4,0},{5,1},{6,2},{7,3},{8,12},{9,13},{10,... | collective-permute-start | bytes 1179656 | tf_op jit(solution)/shard_map/ppermute | solution.py:134
  109.8 25.0 %collective-permute-start.13 = (bf16[4,2,64,384]{3,2,1,0:T(8,128)(2,1)S(1)}, bf16[4,2,64,384]{3,2,1,0:T(8,128)(2,1)S(1)}, u32[]{:S(2)}, u32[]{:S(2)}) collective-permute-start(bf16[4,2,64,384]{3,2,1,0:T(8,128)(2,1)S(1)} %get-tuple-element.51), channel_id=1, source_target_pairs={{0,2},{1,3},{2,4},{3,5},{4,6},{5,7},{6,0},{7,1},{8,14},{9,15},{10,... | collective-permute-start | bytes 1179656 | tf_op jit(solution)/shard_map/ppermute | solution.py:134
  109.8 62.6 %collective-permute-start.9 = (bf16[4,2,64,384]{3,2,1,0:T(8,128)(2,1)}, bf16[4,2,64,384]{3,2,1,0:T(8,128)(2,1)S(1)}, u32[]{:S(2)}, u32[]{:S(2)}) collective-permute-start(bf16[4,2,64,384]{3,2,1,0:T(8,128)(2,1)} %get-tuple-element.46), channel_id=1, source_target_pairs={{0,6},{1,7},{2,0},{3,1},{4,2},{5,3},{6,4},{7,5},{8,10},{9,11},{10,... | collective-permute-start | bytes 1179656 | tf_op jit(solution)/shard_map/ppermute | solution.py:134
  113.4 41.6 %collective-permute-start.14 = (bf16[4,2,64,384]{3,2,1,0:T(8,128)(2,1)S(1)}, bf16[4,2,64,384]{3,2,1,0:T(8,128)(2,1)S(1)}, u32[]{:S(2)}, u32[]{:S(2)}) collective-permute-start(bf16[4,2,64,384]{3,2,1,0:T(8,128)(2,1)S(1)} %get-tuple-element.52), channel_id=1, source_target_pairs={{0,5},{1,4},{2,7},{3,6},{4,1},{5,0},{6,3},{7,2},{8,13},{9,12},{10,... | collective-permute-start | bytes 1179656 | tf_op jit(solution)/shard_map/ppermute | solution.py:134
  116.0 43.8 %collective-permute-start.15 = (bf16[4,2,64,384]{3,2,1,0:T(8,128)(2,1)S(1)}, bf16[4,2,64,384]{3,2,1,0:T(8,128)(2,1)S(1)}, u32[]{:S(2)}, u32[]{:S(2)}) collective-permute-start(bf16[4,2,64,384]{3,2,1,0:T(8,128)(2,1)S(1)} %get-tuple-element.53), channel_id=1, source_target_pairs={{0,3},{1,2},{2,5},{3,4},{4,7},{5,6},{6,1},{7,0},{8,15},{9,14},{10,... | collective-permute-start | bytes 1179656 | tf_op jit(solution)/shard_map/ppermute | solution.py:134
  127.4 32.5 %copy-start.10 = (bf16[4,2,64,384]{3,2,1,0:T(8,128)(2,1)}, bf16[4,2,64,384]{3,2,1,0:T(8,128)(2,1)S(1)}, u32[]{:S(2)}) copy-start(bf16[4,2,64,384]{3,2,1,0:T(8,128)(2,1)S(1)} %collective-permute-done.12.refs_1_) | copy-start | bytes 1179652
  127.4 53.5 %collective-permute-start.10 = (bf16[4,2,64,384]{3,2,1,0:T(8,128)(2,1)}, bf16[4,2,64,384]{3,2,1,0:T(8,128)(2,1)S(1)}, u32[]{:S(2)}, u32[]{:S(2)}) collective-permute-start(bf16[4,2,64,384]{3,2,1,0:T(8,128)(2,1)} %get-tuple-element.47), channel_id=1, source_target_pairs={{0,7},{1,6},{2,1},{3,0},{4,3},{5,2},{6,5},{7,4},{8,11},{9,10},{10,... | collective-permute-start | bytes 1179656 | tf_op jit(solution)/shard_map/ppermute | solution.py:134
  134.8 25.1 %copy-start.11 = (bf16[4,2,64,384]{3,2,1,0:T(8,128)(2,1)}, bf16[4,2,64,384]{3,2,1,0:T(8,128)(2,1)S(1)}, u32[]{:S(2)}) copy-start(bf16[4,2,64,384]{3,2,1,0:T(8,128)(2,1)S(1)} %collective-permute-done.13.refs_2_) | copy-start | bytes 1179652
  134.8 46.1 %collective-permute-start.11 = (bf16[4,2,64,384]{3,2,1,0:T(8,128)(2,1)S(1)}, bf16[4,2,64,384]{3,2,1,0:T(8,128)(2,1)S(1)}, u32[]{:S(2)}, u32[]{:S(2)}) collective-permute-start(bf16[4,2,64,384]{3,2,1,0:T(8,128)(2,1)S(1)} %get-tuple-element.48), channel_id=1, source_target_pairs={{0,1},{1,0},{2,3},{3,2},{4,5},{5,4},{6,7},{7,6},{8,9},{9,8},{10,11... | collective-permute-start | bytes 1179656 | tf_op jit(solution)/shard_map/ppermute | solution.py:134
  155.0 4.9 %copy-start.12 = (bf16[4,2,64,384]{3,2,1,0:T(8,128)(2,1)}, bf16[4,2,64,384]{3,2,1,0:T(8,128)(2,1)S(1)}, u32[]{:S(2)}) copy-start(bf16[4,2,64,384]{3,2,1,0:T(8,128)(2,1)S(1)} %collective-permute-done.14.refs_3_) | copy-start | bytes 1179652
  159.9 0.8 copy-start.13
  172.4 8.4 %copy-start.7 = (bf16[4,2,64,384]{3,2,1,0:T(8,128)(2,1)}, bf16[4,2,64,384]{3,2,1,0:T(8,128)(2,1)S(1)}, u32[]{:S(2)}) copy-start(bf16[4,2,64,384]{3,2,1,0:T(8,128)(2,1)S(1)} %collective-permute-done.9.refs_0_) | copy-start | bytes 1179652
  180.9 0.7 copy-start.8
  180.9 0.9 copy-start.9

commit v2 on v1

--- a/solution.py
+++ b/solution.py
@@ -13,7 +13,7 @@
 NEGATIVE = -1e30
 LOG2E = 1.4426950408889634
 CORES = 2
-ORDER = (4, 6, 5, 7, 2, 3, 1)
+ORDER = (4, 6, 5, 7, 1, 2, 3)
 CHUNKS = ((0, 3),)
 ANY = pl.BlockSpec(memory_space=pl.ANY)
 VMEM = pl.BlockSpec(memory_space=pltpu.VMEM)

time: 188 us -> 187 us (level)
  the two profiles are of different devices: /device:TPU:31 before, /device:TPU:33 now
where the time goes in v2:
time: 187 us; the launch traced here: 183 us
  waiting for transfers between devices  116 us (62%)
  starting transfers between devices  36.9 us (20%)
  Pallas kernels  19.4 us (10%)
  local copies, waits for them, and re-layouts  8.99 us (5%)
  between operations  2.18 us (1%)
    ppermute x14, waiting for transfers between devices, exchange(): received[k] = lax.ppermute(parts[k], ('dp', 'seq'), pairs)  105 us
    ppermute x14, starting transfers between devices, exchange(): received[k] = lax.ppermute(parts[k], ('dp', 'seq'), pairs)  36.9 us
    ppermute x1, waiting for transfers between devices, swap(): lax.ppermute(gift, 'dp', pairs)  10.7 us
    unnamed x37, local copies, waits for them, and re-layouts  6.99 us
    pallas_call x1, Pallas kernels, backward(): pl.pallas_call(backward_kernel, out_shape=[jax.ShapeDtypeStruct(parts[0]....  5.72 us
    pallas_call x2, Pallas kernels, unpack(): pl.pallas_call(functools.partial(unpack_kernel, chunk, steps), out_shape=...  5.25 us
  transfers between devices with their start and end apart: 15, of which 11 were waited for; matrix products, arithmetic and copies ran while one was open for 2% of the time, Pallas kernels for 3%

profile of v2, /device:TPU:33, one launch (start us, length us, event | category | flops | bytes accessed | tf_op | source)
XLA Modules:
  0.0 183.3 jit_solution(17722677595365347339)
XLA Ops:
  0.7 2.9 %pack.1 = (bf16[4,2,64,384]{3,2,1,0:T(8,128)(2,1)}, bf16[4,2,64,384]{3,2,1,0:T(8,128)(2,1)}, bf16[4,2,64,384]{3,2,1,0:T(8,128)(2,1)}, bf16[4,2,64,384]{3,2,1,0:T...) custom-call(bf16[3,1,2,64,3072]{4,3,2,1,0:T(8,128)(2,1)} %qkv.1, ...), custom_call_target="tpu_custom_call" | custom-call | tf_op jit(solution)/shard_map/pack/pallas_call | solution.py:112
  4.3 5.1 %collective-permute-start.3 = (bf16[4,2,64,384]{3,2,1,0:T(8,128)(2,1)}, bf16[4,2,64,384]{3,2,1,0:T(8,128)(2,1)S(1)}, u32[]{:S(2)}, u32[]{:S(2)}) collective-permute-start(bf16[4,2,64,384]{3,2,1,0:T(8,128)(2,1)} %get-tuple-element.36), channel_id=1, source_target_pairs={{0,2},{1,3},{2,4},{3,5},{4,6},{5,7},{6,0},{7,1},{8,14},{9,15},{10,... | collective-permute-start | bytes 1179656 | tf_op jit(solution)/shard_map/ppermute | solution.py:134
  9.4 1.4 collective-permute-start.4
  10.9 5.7 %collective-permute-start.6 = (bf16[4,2,64,384]{3,2,1,0:T(8,128)(2,1)}, bf16[4,2,64,384]{3,2,1,0:T(8,128)(2,1)S(1)}, u32[]{:S(2)}, u32[]{:S(2)}) collective-permute-start(bf16[4,2,64,384]{3,2,1,0:T(8,128)(2,1)} %get-tuple-element.39), channel_id=1, source_target_pairs={{0,5},{1,4},{2,7},{3,6},{4,1},{5,0},{6,3},{7,2},{8,13},{9,12},{10,... | collective-permute-start | bytes 1179656 | tf_op jit(solution)/shard_map/ppermute | solution.py:134
  16.6 1.2 collective-permute-start.7
  18.2 3.3 %collective-permute-start.8 = (bf16[4,2,64,384]{3,2,1,0:T(8,128)(2,1)}, bf16[4,2,64,384]{3,2,1,0:T(8,128)(2,1)S(1)}, u32[]{:S(2)}, u32[]{:S(2)}) collective-permute-start(bf16[4,2,64,384]{3,2,1,0:T(8,128)(2,1)} %get-tuple-element.41), channel_id=1, source_target_pairs={{0,7},{1,6},{2,1},{3,0},{4,3},{5,2},{6,5},{7,4},{8,11},{9,10},{10,... | collective-permute-start | bytes 1179656 | tf_op jit(solution)/shard_map/ppermute | solution.py:134
  23.6 2.0 %plan.1 = s32[10]{0:T(128)} custom-call(s32[32,2]{1,0:T(8,128)} %copy.9.lengths, s32[32,2]{1,0:T(8,128)} %copy.10.to_group, s32[32,2]{1,0:T(8,128)} %copy.11.to_slot), custom_call_target="tpu_custom_call" | custom-call | tf_op jit(solution)/shard_map/plan/pallas_call | solution.py:59
  25.7 1.3 fusion
  28.2 2.1 %collective-permute-done.4.refs_3_ = bf16[4,2,64,384]{3,2,1,0:T(8,128)(2,1)S(1)} collective-permute-done((bf16[4,2,64,384]{3,2,1,0:T(8,128)(2,1)}, bf16[4,2,64,384]{3,2,1,0:T(8,128)(2,1)S(1)}, u32[]{:S(2)}, u32[]{:S(2)}) %collective-permute-start.4) | collective-permute-done | bytes 393248 | tf_op jit(solution)/shard_map/ppermute | solution.py:134
  30.3 40.3 %collective-permute-done.5.refs_4_ = bf16[4,2,64,384]{3,2,1,0:T(8,128)(2,1)S(1)} collective-permute-done((bf16[4,2,64,384]{3,2,1,0:T(8,128)(2,1)}, bf16[4,2,64,384]{3,2,1,0:T(8,128)(2,1)S(1)}, u32[]{:S(2)}, u32[]{:S(2)}) %collective-permute-start.5) | collective-permute-done | bytes 393248 | tf_op jit(solution)/shard_map/ppermute | solution.py:134
  70.6 8.7 %collective-permute-done.6.refs_5_ = bf16[4,2,64,384]{3,2,1,0:T(8,128)(2,1)S(1)} collective-permute-done((bf16[4,2,64,384]{3,2,1,0:T(8,128)(2,1)}, bf16[4,2,64,384]{3,2,1,0:T(8,128)(2,1)S(1)}, u32[]{:S(2)}, u32[]{:S(2)}) %collective-permute-start.6) | collective-permute-done | bytes 393248 | tf_op jit(solution)/shard_map/ppermute | solution.py:134
  79.3 1.1 copy-done
  81.0 3.5 %forward.1 = (bf16[2,512,384]{2,1,0:T(8,128)(2,1)S(1)}, f32[2,8,512]{2,1,0:T(8,128)S(1)}, bf16[512,384]{1,0:T(8,128)(2,1)}, bf16[512,384]{1,0:T(8,128)(2,1)}) custom-call(s32[10]{0:T(128)S(1)} %copy-done.5, bf16[4,2,64,384]{3,2,1,0:T(8,128)(2,1)S(1)} %copy-done, bf16[4,2,64,384]{3,2,1,0:T(8,128)(2,1)S(1)} %collective-permute-done.2.refs_1_, ...), custom_call_target="tpu_custom_call" | custom-call | tf_op jit(solution)/shard_map/forward/pallas_call | solution.py:224
  84.5 0.9 copy-done.3
  85.4 11.5 %conditional.2 = (bf16[512,384]{1,0:T(8,128)(2,1)}) conditional(s32[]{:T(128)} %bitcast, bf16[512,384]{1,0:T(8,128)(2,1)} %get-tuple-element.44, bf16[512,384]{1,0:T(8,128)(2,1)} %get-tuple-element.44), branch_computations={%region_0.0_spmd, %region_1.0_spmd} | conditional | bytes 2359344 | solution.py:353
  85.4 10.7 %collective-permute-done = bf16[512,384]{1,0:T(8,128)(2,1)S(1)} collective-permute-done((bf16[512,384]{1,0:T(8,128)(2,1)}, bf16[512,384]{1,0:T(8,128)(2,1)S(1)}, u32[]{:S(2)}, u32[]{:S(2)}) %collective-permute-start) | collective-permute-done | bytes 393248 | tf_op jit(solution)/shard_map/cond/branch_1_fun/ppermute | solution.py:354
  96.9 5.7 %backward.1 = (bf16[4,2,64,384]{3,2,1,0:T(8,128)(2,1)S(1)}, bf16[4,2,64,384]{3,2,1,0:T(8,128)(2,1)}, bf16[4,2,64,384]{3,2,1,0:T(8,128)(2,1)}, bf16[4,2,64,384]{3...) custom-call(s32[10]{0:T(128)S(1)} %copy-done.6, ...), custom_call_target="tpu_custom_call" | custom-call | tf_op jit(solution)/shard_map/backward/pallas_call | solution.py:303
  103.3 4.2 %collective-permute-start.12 = (bf16[4,2,64,384]{3,2,1,0:T(8,128)(2,1)S(1)}, bf16[4,2,64,384]{3,2,1,0:T(8,128)(2,1)S(1)}, u32[]{:S(2)}, u32[]{:S(2)}) collective-permute-start(bf16[4,2,64,384]{3,2,1,0:T(8,128)(2,1)S(1)} %get-tuple-element.50), channel_id=1, source_target_pairs={{0,4},{1,5},{2,6},{3,7},{4,0},{5,1},{6,2},{7,3},{8,12},{9,13},{10,... | collective-permute-start | bytes 1179656 | tf_op jit(solution)/shard_map/ppermute | solution.py:134
  107.5 1.2 collective-permute-start.13
  108.7 1.5 collective-permute-start.9
  110.2 4.3 %collective-permute-start.14 = (bf16[4,2,64,384]{3,2,1,0:T(8,128)(2,1)S(1)}, bf16[4,2,64,384]{3,2,1,0:T(8,128)(2,1)S(1)}, u32[]{:S(2)}, u32[]{:S(2)}) collective-permute-start(bf16[4,2,64,384]{3,2,1,0:T(8,128)(2,1)S(1)} %get-tuple-element.52), channel_id=1, source_target_pairs={{0,5},{1,4},{2,7},{3,6},{4,1},{5,0},{6,3},{7,2},{8,13},{9,12},{10,... | collective-permute-start | bytes 1179656 | tf_op jit(solution)/shard_map/ppermute | solution.py:134
  115.0 6.3 %collective-permute-done.12.refs_1_ = bf16[4,2,64,384]{3,2,1,0:T(8,128)(2,1)S(1)} collective-permute-done((bf16[4,2,64,384]{3,2,1,0:T(8,128)(2,1)S(1)}, bf16[4,2,64,384]{3,2,1,0:T(8,128)(2,1)S(1)}, u32[]{:S(2)}, u32[]{:S(2)}) %collective-permute-start.12) | collective-permute-done | bytes 393248 | tf_op jit(solution)/shard_map/ppermute | solution.py:134
  121.3 4.8 %collective-permute-start.10 = (bf16[4,2,64,384]{3,2,1,0:T(8,128)(2,1)}, bf16[4,2,64,384]{3,2,1,0:T(8,128)(2,1)S(1)}, u32[]{:S(2)}, u32[]{:S(2)}) collective-permute-start(bf16[4,2,64,384]{3,2,1,0:T(8,128)(2,1)} %get-tuple-element.47), channel_id=1, source_target_pairs={{0,6},{1,7},{2,0},{3,1},{4,2},{5,3},{6,4},{7,5},{8,10},{9,11},{10,... | collective-permute-start | bytes 1179656 | tf_op jit(solution)/shard_map/ppermute | solution.py:134
  126.2 9.5 %collective-permute-done.13.refs_2_ = bf16[4,2,64,384]{3,2,1,0:T(8,128)(2,1)S(1)} collective-permute-done((bf16[4,2,64,384]{3,2,1,0:T(8,128)(2,1)S(1)}, bf16[4,2,64,384]{3,2,1,0:T(8,128)(2,1)S(1)}, u32[]{:S(2)}, u32[]{:S(2)}) %collective-permute-start.13) | collective-permute-done | bytes 393248 | tf_op jit(solution)/shard_map/ppermute | solution.py:134
  135.7 2.8 %collective-permute-start.11 = (bf16[4,2,64,384]{3,2,1,0:T(8,128)(2,1)S(1)}, bf16[4,2,64,384]{3,2,1,0:T(8,128)(2,1)S(1)}, u32[]{:S(2)}, u32[]{:S(2)}) collective-permute-start(bf16[4,2,64,384]{3,2,1,0:T(8,128)(2,1)S(1)} %get-tuple-element.48), channel_id=1, source_target_pairs={{0,7},{1,6},{2,1},{3,0},{4,3},{5,2},{6,5},{7,4},{8,11},{9,10},{10,... | collective-permute-start | bytes 1179656 | tf_op jit(solution)/shard_map/ppermute | solution.py:134
  138.5 14.1 %collective-permute-done.14.refs_3_ = bf16[4,2,64,384]{3,2,1,0:T(8,128)(2,1)S(1)} collective-permute-done((bf16[4,2,64,384]{3,2,1,0:T(8,128)(2,1)S(1)}, bf16[4,2,64,384]{3,2,1,0:T(8,128)(2,1)S(1)}, u32[]{:S(2)}, u32[]{:S(2)}) %collective-permute-start.14) | collective-permute-done | bytes 393248 | tf_op jit(solution)/shard_map/ppermute | solution.py:134
  152.6 8.2 %collective-permute-done.15.refs_4_ = bf16[4,2,64,384]{3,2,1,0:T(8,128)(2,1)S(1)} collective-permute-done((bf16[4,2,64,384]{3,2,1,0:T(8,128)(2,1)S(1)}, bf16[4,2,64,384]{3,2,1,0:T(8,128)(2,1)S(1)}, u32[]{:S(2)}, u32[]{:S(2)}) %collective-permute-start.15) | collective-permute-done | bytes 393248 | tf_op jit(solution)/shard_map/ppermute | solution.py:134
  160.8 0.8 copy-done.13
  161.5 2.9 %unpack.2 = (bf16[1,2,64,3072]{3,2,1,0:T(8,128)(2,1)}, bf16[3,1,2,64,3072]{4,3,2,1,0:T(8,128)(2,1)}) custom-call(bf16[4,2,64,384]{3,2,1,0:T(8,128)(2,1)} %copy-done.4, bf16[4,2,64,384]{3,2,1,0:T(8,128)(2,1)} %copy-done.10, bf16[4,2,64,384]{3,2,1,0:T(8,128)(2,1)} %copy-done.11, bf16[4,2,64,384]{3,2,1,0:T(8,128)(2,1)} %copy-done.12, ...), custom_call_target="tpu_custom_call" | custom-call | tf_op jit(solution)/shard_map/unpack/pallas_call | solution.py:335
  164.4 7.2 %collective-permute-done.10.refs_1_ = bf16[4,2,64,384]{3,2,1,0:T(8,128)(2,1)S(1)} collective-permute-done((bf16[4,2,64,384]{3,2,1,0:T(8,128)(2,1)}, bf16[4,2,64,384]{3,2,1,0:T(8,128)(2,1)S(1)}, u32[]{:S(2)}, u32[]{:S(2)}) %collective-permute-start.10) | collective-permute-done | bytes 393248 | tf_op jit(solution)/shard_map/ppermute | solution.py:134
  171.6 8.4 %collective-permute-done.11.refs_2_ = bf16[4,2,64,384]{3,2,1,0:T(8,128)(2,1)S(1)} collective-permute-done((bf16[4,2,64,384]{3,2,1,0:T(8,128)(2,1)S(1)}, bf16[4,2,64,384]{3,2,1,0:T(8,128)(2,1)S(1)}, u32[]{:S(2)}, u32[]{:S(2)}) %collective-permute-start.11) | collective-permute-done | bytes 393248 | tf_op jit(solution)/shard_map/ppermute | solution.py:134
  180.8 2.4 %unpack.3 = (bf16[1,2,64,3072]{3,2,1,0:T(8,128)(2,1)}, bf16[3,1,2,64,3072]{4,3,2,1,0:T(8,128)(2,1)}) custom-call(bf16[4,2,64,384]{3,2,1,0:T(8,128)(2,1)} %copy-done.7, bf16[4,2,64,384]{3,2,1,0:T(8,128)(2,1)} %copy-done.8, bf16[4,2,64,384]{3,2,1,0:T(8,128)(2,1)} %copy-done.9, ...), custom_call_target="tpu_custom_call", output_to_operand_aliasing={{0}: (3, {}), {1}: (4, {})} | custom-call | tf_op jit(solution)/shard_map/unpack/pallas_call | solution.py:335
  (45 shorter events, 6.7 us)
Async XLA Ops:
  0.6 20.9 %copy-start.14 = (s32[32,2]{0,1:T(2,128)S(1)}, s32[32,2]{0,1:T(2,128)}, u32[]{:S(2)}) copy-start(s32[32,2]{0,1:T(2,128)} %param.11) | copy-start | bytes 772
  0.6 21.6 %copy-start.15 = (s32[32,2]{0,1:T(2,128)S(1)}, s32[32,2]{0,1:T(2,128)}, u32[]{:S(2)}) copy-start(s32[32,2]{0,1:T(2,128)} %param.12) | copy-start | bytes 772
  0.7 22.3 %copy-start.16 = (s32[32,2]{0,1:T(2,128)S(1)}, s32[32,2]{0,1:T(2,128)}, u32[]{:S(2)}) copy-start(s32[32,2]{0,1:T(2,128)} %param.13) | copy-start | bytes 772
  3.5 13.0 %collective-permute-start.2 = (bf16[4,2,64,384]{3,2,1,0:T(8,128)(2,1)}, bf16[4,2,64,384]{3,2,1,0:T(8,128)(2,1)S(1)}, u32[]{:S(2)}, u32[]{:S(2)}) collective-permute-start(bf16[4,2,64,384]{3,2,1,0:T(8,128)(2,1)} %get-tuple-element.35), channel_id=1, source_target_pairs={{0,1},{1,0},{2,3},{3,2},{4,5},{5,4},{6,7},{7,6},{8,9},{9,8},{10,11... | collective-permute-start | bytes 1179656 | tf_op jit(solution)/shard_map/ppermute | solution.py:134
  4.3 13.9 %collective-permute-start.3 = (bf16[4,2,64,384]{3,2,1,0:T(8,128)(2,1)}, bf16[4,2,64,384]{3,2,1,0:T(8,128)(2,1)S(1)}, u32[]{:S(2)}, u32[]{:S(2)}) collective-permute-start(bf16[4,2,64,384]{3,2,1,0:T(8,128)(2,1)} %get-tuple-element.36), channel_id=1, source_target_pairs={{0,2},{1,3},{2,4},{3,5},{4,6},{5,7},{6,0},{7,1},{8,14},{9,15},{10,... | collective-permute-start | bytes 1179656 | tf_op jit(solution)/shard_map/ppermute | solution.py:134
  9.4 20.9 %collective-permute-start.4 = (bf16[4,2,64,384]{3,2,1,0:T(8,128)(2,1)}, bf16[4,2,64,384]{3,2,1,0:T(8,128)(2,1)S(1)}, u32[]{:S(2)}, u32[]{:S(2)}) collective-permute-start(bf16[4,2,64,384]{3,2,1,0:T(8,128)(2,1)} %get-tuple-element.37), channel_id=1, source_target_pairs={{0,3},{1,2},{2,5},{3,4},{4,7},{5,6},{6,1},{7,0},{8,15},{9,14},{10,... | collective-permute-start | bytes 1179656 | tf_op jit(solution)/shard_map/ppermute | solution.py:134
  10.9 59.8 %collective-permute-start.5 = (bf16[4,2,64,384]{3,2,1,0:T(8,128)(2,1)}, bf16[4,2,64,384]{3,2,1,0:T(8,128)(2,1)S(1)}, u32[]{:S(2)}, u32[]{:S(2)}) collective-permute-start(bf16[4,2,64,384]{3,2,1,0:T(8,128)(2,1)} %get-tuple-element.38), channel_id=1, source_target_pairs={{0,4},{1,5},{2,6},{3,7},{4,0},{5,1},{6,2},{7,3},{8,12},{9,13},{10,... | collective-permute-start | bytes 1179656 | tf_op jit(solution)/shard_map/ppermute | solution.py:134
  10.9 68.4 %collective-permute-start.6 = (bf16[4,2,64,384]{3,2,1,0:T(8,128)(2,1)}, bf16[4,2,64,384]{3,2,1,0:T(8,128)(2,1)S(1)}, u32[]{:S(2)}, u32[]{:S(2)}) collective-permute-start(bf16[4,2,64,384]{3,2,1,0:T(8,128)(2,1)} %get-tuple-element.39), channel_id=1, source_target_pairs={{0,5},{1,4},{2,7},{3,6},{4,1},{5,0},{6,3},{7,2},{8,13},{9,12},{10,... | collective-permute-start | bytes 1179656 | tf_op jit(solution)/shard_map/ppermute | solution.py:134
  16.6 62.7 %collective-permute-start.7 = (bf16[4,2,64,384]{3,2,1,0:T(8,128)(2,1)}, bf16[4,2,64,384]{3,2,1,0:T(8,128)(2,1)S(1)}, u32[]{:S(2)}, u32[]{:S(2)}) collective-permute-start(bf16[4,2,64,384]{3,2,1,0:T(8,128)(2,1)} %get-tuple-element.40), channel_id=1, source_target_pairs={{0,6},{1,7},{2,0},{3,1},{4,2},{5,3},{6,4},{7,5},{8,10},{9,11},{10,... | collective-permute-start | bytes 1179656 | tf_op jit(solution)/shard_map/ppermute | solution.py:134
  18.2 61.1 %collective-permute-start.8 = (bf16[4,2,64,384]{3,2,1,0:T(8,128)(2,1)}, bf16[4,2,64,384]{3,2,1,0:T(8,128)(2,1)S(1)}, u32[]{:S(2)}, u32[]{:S(2)}) collective-permute-start(bf16[4,2,64,384]{3,2,1,0:T(8,128)(2,1)} %get-tuple-element.41), channel_id=1, source_target_pairs={{0,7},{1,6},{2,1},{3,0},{4,3},{5,2},{6,5},{7,4},{8,11},{9,10},{10,... | collective-permute-start | bytes 1179656 | tf_op jit(solution)/shard_map/ppermute | solution.py:134
  79.3 17.6 %copy-start.2 = (bf16[4,2,64,384]{3,2,1,0:T(8,128)(2,1)}, bf16[4,2,64,384]{3,2,1,0:T(8,128)(2,1)S(1)}, u32[]{:S(2)}) copy-start(bf16[4,2,64,384]{3,2,1,0:T(8,128)(2,1)S(1)} %collective-permute-done.8.refs_7_) | copy-start | bytes 1179652
  79.3 1.1 copy-start
  80.4 0.6 copy-start.5
  81.0 15.8 %copy-start.1 = (bf16[4,2,64,384]{3,2,1,0:T(8,128)(2,1)S(1)}, bf16[4,2,64,384]{3,2,1,0:T(8,128)(2,1)}, u32[]{:S(2)}) copy-start(bf16[4,2,64,384]{3,2,1,0:T(8,128)(2,1)} %get-tuple-element.34.refs_0_) | copy-start | bytes 1179652
  81.0 15.8 %copy-start.6 = (s32[10]{0:T(128)S(1)}, s32[10]{0:T(128)}, u32[]{:S(2)}) copy-start(s32[10]{0:T(128)} %plan.1) | copy-start | bytes 124
  84.5 0.9 copy-start.3
  85.4 10.7 %collective-permute-start = (bf16[512,384]{1,0:T(8,128)(2,1)}, bf16[512,384]{1,0:T(8,128)(2,1)S(1)}, u32[]{:S(2)}, u32[]{:S(2)}) collective-permute-start(bf16[512,384]{1,0:T(8,128)(2,1)} %param.1), channel_id=1, source_target_pairs={{0,8},{8,0},{16,24},{24,16},{32,40},{40,32},{48,56},{56,48},{64,72... | collective-permute-start | bytes 1179656 | tf_op jit(solution)/shard_map/cond/branch_1_fun/ppermute | solution.py:354
  102.6 0.8 copy-start.4
  103.3 18.0 %collective-permute-start.12 = (bf16[4,2,64,384]{3,2,1,0:T(8,128)(2,1)S(1)}, bf16[4,2,64,384]{3,2,1,0:T(8,128)(2,1)S(1)}, u32[]{:S(2)}, u32[]{:S(2)}) collective-permute-start(bf16[4,2,64,384]{3,2,1,0:T(8,128)(2,1)S(1)} %get-tuple-element.50), channel_id=1, source_target_pairs={{0,4},{1,5},{2,6},{3,7},{4,0},{5,1},{6,2},{7,3},{8,12},{9,13},{10,... | collective-permute-start | bytes 1179656 | tf_op jit(solution)/shard_map/ppermute | solution.py:134
  107.5 28.2 %collective-permute-start.13 = (bf16[4,2,64,384]{3,2,1,0:T(8,128)(2,1)S(1)}, bf16[4,2,64,384]{3,2,1,0:T(8,128)(2,1)S(1)}, u32[]{:S(2)}, u32[]{:S(2)}) collective-permute-start(bf16[4,2,64,384]{3,2,1,0:T(8,128)(2,1)S(1)} %get-tuple-element.51), channel_id=1, source_target_pairs={{0,2},{1,3},{2,4},{3,5},{4,6},{5,7},{6,0},{7,1},{8,14},{9,15},{10,... | collective-permute-start | bytes 1179656 | tf_op jit(solution)/shard_map/ppermute | solution.py:134
  108.7 55.7 %collective-permute-start.9 = (bf16[4,2,64,384]{3,2,1,0:T(8,128)(2,1)}, bf16[4,2,64,384]{3,2,1,0:T(8,128)(2,1)S(1)}, u32[]{:S(2)}, u32[]{:S(2)}) collective-permute-start(bf16[4,2,64,384]{3,2,1,0:T(8,128)(2,1)} %get-tuple-element.46), channel_id=1, source_target_pairs={{0,1},{1,0},{2,3},{3,2},{4,5},{5,4},{6,7},{7,6},{8,9},{9,8},{10,11... | collective-permute-start | bytes 1179656 | tf_op jit(solution)/shard_map/ppermute | solution.py:134
  110.2 42.4 %collective-permute-start.14 = (bf16[4,2,64,384]{3,2,1,0:T(8,128)(2,1)S(1)}, bf16[4,2,64,384]{3,2,1,0:T(8,128)(2,1)S(1)}, u32[]{:S(2)}, u32[]{:S(2)}) collective-permute-start(bf16[4,2,64,384]{3,2,1,0:T(8,128)(2,1)S(1)} %get-tuple-element.52), channel_id=1, source_target_pairs={{0,5},{1,4},{2,7},{3,6},{4,1},{5,0},{6,3},{7,2},{8,13},{9,12},{10,... | collective-permute-start | bytes 1179656 | tf_op jit(solution)/shard_map/ppermute | solution.py:134
  114.5 46.3 %collective-permute-start.15 = (bf16[4,2,64,384]{3,2,1,0:T(8,128)(2,1)S(1)}, bf16[4,2,64,384]{3,2,1,0:T(8,128)(2,1)S(1)}, u32[]{:S(2)}, u32[]{:S(2)}) collective-permute-start(bf16[4,2,64,384]{3,2,1,0:T(8,128)(2,1)S(1)} %get-tuple-element.53), channel_id=1, source_target_pairs={{0,3},{1,2},{2,5},{3,4},{4,7},{5,6},{6,1},{7,0},{8,15},{9,14},{10,... | collective-permute-start | bytes 1179656 | tf_op jit(solution)/shard_map/ppermute | solution.py:134
  121.3 39.4 %copy-start.10 = (bf16[4,2,64,384]{3,2,1,0:T(8,128)(2,1)}, bf16[4,2,64,384]{3,2,1,0:T(8,128)(2,1)S(1)}, u32[]{:S(2)}) copy-start(bf16[4,2,64,384]{3,2,1,0:T(8,128)(2,1)S(1)} %collective-permute-done.12.refs_1_) | copy-start | bytes 1179652
  121.3 50.3 %collective-permute-start.10 = (bf16[4,2,64,384]{3,2,1,0:T(8,128)(2,1)}, bf16[4,2,64,384]{3,2,1,0:T(8,128)(2,1)S(1)}, u32[]{:S(2)}, u32[]{:S(2)}) collective-permute-start(bf16[4,2,64,384]{3,2,1,0:T(8,128)(2,1)} %get-tuple-element.47), channel_id=1, source_target_pairs={{0,6},{1,7},{2,0},{3,1},{4,2},{5,3},{6,4},{7,5},{8,10},{9,11},{10,... | collective-permute-start | bytes 1179656 | tf_op jit(solution)/shard_map/ppermute | solution.py:134
  135.7 25.1 %copy-start.11 = (bf16[4,2,64,384]{3,2,1,0:T(8,128)(2,1)}, bf16[4,2,64,384]{3,2,1,0:T(8,128)(2,1)S(1)}, u32[]{:S(2)}) copy-start(bf16[4,2,64,384]{3,2,1,0:T(8,128)(2,1)S(1)} %collective-permute-done.13.refs_2_) | copy-start | bytes 1179652
  135.7 44.3 %collective-permute-start.11 = (bf16[4,2,64,384]{3,2,1,0:T(8,128)(2,1)S(1)}, bf16[4,2,64,384]{3,2,1,0:T(8,128)(2,1)S(1)}, u32[]{:S(2)}, u32[]{:S(2)}) collective-permute-start(bf16[4,2,64,384]{3,2,1,0:T(8,128)(2,1)S(1)} %get-tuple-element.48), channel_id=1, source_target_pairs={{0,7},{1,6},{2,1},{3,0},{4,3},{5,2},{6,5},{7,4},{8,11},{9,10},{10,... | collective-permute-start | bytes 1179656 | tf_op jit(solution)/shard_map/ppermute | solution.py:134
  152.6 8.2 %copy-start.12 = (bf16[4,2,64,384]{3,2,1,0:T(8,128)(2,1)}, bf16[4,2,64,384]{3,2,1,0:T(8,128)(2,1)S(1)}, u32[]{:S(2)}) copy-start(bf16[4,2,64,384]{3,2,1,0:T(8,128)(2,1)S(1)} %collective-permute-done.14.refs_3_) | copy-start | bytes 1179652
  160.8 0.8 copy-start.13
  164.4 15.6 %copy-start.7 = (bf16[4,2,64,384]{3,2,1,0:T(8,128)(2,1)}, bf16[4,2,64,384]{3,2,1,0:T(8,128)(2,1)S(1)}, u32[]{:S(2)}) copy-start(bf16[4,2,64,384]{3,2,1,0:T(8,128)(2,1)S(1)} %collective-permute-done.9.refs_0_) | copy-start | bytes 1179652
  171.6 8.4 %copy-start.8 = (bf16[4,2,64,384]{3,2,1,0:T(8,128)(2,1)}, bf16[4,2,64,384]{3,2,1,0:T(8,128)(2,1)S(1)}, u32[]{:S(2)}) copy-start(bf16[4,2,64,384]{3,2,1,0:T(8,128)(2,1)S(1)} %collective-permute-done.10.refs_1_) | copy-start | bytes 1179652
  180.0 0.8 copy-start.9
